TPU v7x, 32 devices: a whole 2x2x4 slice. The times are simulated.
32 devices in a mesh: req: 4 (over y, x), seq: 8 (over z, core).
Axes of the slice: x: 2, y: 2, z: 4, core: 2. Of those that a mesh axis runs over, the one named last changes fastest.
Arguments:
- new_tokens: bfloat16 [32, 4, 2048], P('req'), may hold values from -6 to 6
- norm_gain: float32 [2048], replicated, may hold values from 0.5 to 1.5
- w_query: bfloat16 [2048, 2048], P(None, 'req'), may hold values from -0.25 to 0.25
- w_key: bfloat16 [2048, 1024], P(None, 'req'), may hold values from -0.125 to 0.125
- w_value: bfloat16 [2048, 1024], P(None, 'req'), may hold values from -0.125 to 0.125
- w_out: bfloat16 [2048, 2048], P('req'), may hold values from -0.125 to 0.125
- pool_keys: bfloat16 [4096, 16, 1024], P(('req', 'seq')), may hold values from -1000 to 1000
- pool_values: bfloat16 [4096, 16, 1024], P(('req', 'seq')), may hold values from -6 to 6
- cache_lengths: int32 [32], replicated, may hold values from 2 to 2044, as said below
- owner: int32 [32], replicated, may hold values from 0 to 31, as said below
- page_table: int32 [32, 128], replicated, may hold values from 0 to 4095, as said below
Outputs:
- out_hidden: bfloat16 [32, 4, 2048], P('req')
- keys_out: bfloat16 [32, 2048, 1024], P('req', 'seq')
- values_out: bfloat16 [32, 2048, 1024], P('req', 'seq')
Inputs may be any that keep to these rules, and one draw needn't show every extreme that they name: A permutation: request r goes to owner slot owner[r], held by request group owner[r] // 8. page_table[r, j] is the pool page holding positions j * 16 to (j + 1) * 16 - 1 of request r; every pool page is named exactly once. Pool pages d * 128 to (d + 1) * 128 - 1 lie on device d of req+seq. The home of page j of request r is the device with req index owner[r] // 8 and seq index j // 16; every device's pool pages include exactly 4 pages of every home. `cache_lengths`: 2044 is reached in every draw.
All inputs are finite; a program needn't handle non-finite values.
Results may differ from a plain program's by a relative error of at most 0.015.
Values may be sent and summed in bfloat16 or wider, within the bound.
A program may use at most 128 MiB of HBM per device.

v0:
```python
import math

import jax
import jax.numpy as jnp
from jax import lax
from jax.sharding import PartitionSpec as P

H = 16
KVH = 8
HD = 128


NORM_EPS = 1e-05
ROPE_BASE = 1000000.0
MASKED = -1e30


def rotate(values, places):
    half_dim = values.shape[-1] // 2
    steps_up = jnp.arange(half_dim, dtype=jnp.float32) * (2.0 / values.shape[-1])
    inverse = ROPE_BASE ** (-steps_up)
    angles = places.astype(jnp.float32)[..., None] * inverse
    cosine = jnp.cos(angles)[..., None, :]
    sine_part = jnp.sin(angles)[..., None, :]
    first_half = values[..., :half_dim]
    second_half = values[..., half_dim:]
    return jnp.concatenate(
        [
            first_half * cosine - second_half * sine_part,
            second_half * cosine + first_half * sine_part,
        ],
        axis=-1,
    )


def shards(
    new_tokens,
    norm_gain,
    w_query,
    w_key,
    w_value,
    w_out,
    pool_keys,
    pool_values,
    cache_lengths,
    owner,
    page_table,
):
    req_count = lax.axis_size("req")
    seq_count = lax.axis_size("seq")
    devices = req_count * seq_count
    req_index = lax.axis_index("req")
    seq_index = lax.axis_index("seq")
    device_index = req_index * seq_count + seq_index
    local_reqs, new_count, model_width = new_tokens.shape
    request_total = owner.shape[0]
    pages_dev, page_len, kv_width = pool_keys.shape
    pages_req = page_table.shape[1]
    pages_home = pages_req // seq_count
    positions = pages_home * page_len
    per_peer = pages_dev // devices
    groups = H // KVH
    query_cols = w_query.shape[1]
    key_cols = w_key.shape[1]
    all_requests = jnp.arange(request_total, dtype=jnp.int32)
    slot_request = jnp.zeros((request_total,), jnp.int32).at[owner].set(all_requests)
    slot_lengths = cache_lengths[slot_request]
    my_lengths = lax.dynamic_slice_in_dim(slot_lengths, req_index * local_reqs, local_reqs)
    owner_col = owner[:, None]
    logical = jnp.arange(pages_req, dtype=jnp.int32)[None, :]
    home_index = (
        (owner_col // local_reqs * seq_count + logical // pages_home) * pages_dev
        + owner_col % local_reqs * pages_home
        + logical % pages_home
    )
    pool_total = devices * pages_dev
    home_of_slot = (
        jnp.zeros((pool_total,), jnp.int32).at[page_table.reshape(-1)].set(home_index.reshape(-1))
    )
    slot_of_home = (
        jnp.zeros((pool_total,), jnp.int32).at[home_index.reshape(-1)].set(page_table.reshape(-1))
    )
    held_homes = lax.dynamic_slice_in_dim(home_of_slot, device_index * pages_dev, pages_dev)
    send_order = jnp.argsort(held_homes)
    arrival = (
        lax.dynamic_slice_in_dim(slot_of_home, device_index * pages_dev, pages_dev) // pages_dev
    )
    arrival_order = jnp.argsort(arrival * pages_dev + jnp.arange(pages_dev, dtype=jnp.int32))
    placement = jnp.argsort(arrival_order)
    outgoing = jnp.stack([pool_keys[send_order], pool_values[send_order]], axis=1)
    outgoing = outgoing.reshape(devices, per_peer, 2, page_len, kv_width)
    incoming = lax.all_to_all(outgoing, ("req", "seq"), split_axis=0, concat_axis=0, tiled=True)
    arrived = incoming.reshape(pages_dev, 2, page_len, kv_width)[placement]
    arrived = arrived.reshape(local_reqs, pages_home, 2, page_len, kv_width)
    cache_keys = arrived[:, :, 0].reshape(local_reqs, positions, kv_width)
    cache_values = arrived[:, :, 1].reshape(local_reqs, positions, kv_width)
    tokens_wide = new_tokens.astype(jnp.float32)
    square_mean = jnp.mean(tokens_wide * tokens_wide, axis=-1, keepdims=True)
    normed = (tokens_wide * lax.rsqrt(square_mean + NORM_EPS) * norm_gain).astype(jnp.bfloat16)
    new_index = jnp.arange(new_count, dtype=jnp.int32)
    row_block = lax.all_gather(normed, "req", axis=0, tiled=True)
    row_count = row_block.shape[0]
    flat_rows = row_block.reshape(row_count * new_count, model_width)
    places = slot_lengths[:, None] + new_index[None, :]
    queries_now = jnp.dot(flat_rows, w_query, preferred_element_type=jnp.float32).reshape(
        row_count, new_count, query_cols // HD, HD
    )
    keys_now = jnp.dot(flat_rows, w_key, preferred_element_type=jnp.float32).reshape(
        row_count, new_count, key_cols // HD, HD
    )
    values_now = jnp.dot(flat_rows, w_value, preferred_element_type=jnp.float32).reshape(
        row_count, new_count, key_cols
    )
    queries_now = rotate(queries_now, places).reshape(row_count, new_count, query_cols)
    keys_now = rotate(keys_now, places).reshape(row_count, new_count, key_cols)
    projected = jnp.concatenate([queries_now, keys_now, values_now], axis=-1).astype(jnp.bfloat16)
    owned_rows = lax.all_to_all(projected, "req", split_axis=0, concat_axis=2, tiled=True)
    owned_rows = owned_rows.reshape(local_reqs, new_count, req_count, query_cols + 2 * key_cols)
    queries = owned_rows[..., :query_cols].reshape(local_reqs, new_count, KVH, groups, HD)
    fresh_keys = owned_rows[..., query_cols : query_cols + key_cols].reshape(
        local_reqs, new_count, KVH, HD
    )
    fresh_values = owned_rows[..., query_cols + key_cols :].reshape(local_reqs, new_count, KVH, HD)
    score_scale = 1.0 / math.sqrt(HD)
    grid_keys = cache_keys.reshape(local_reqs, positions, KVH, HD)
    grid_values = cache_values.reshape(local_reqs, positions, KVH, HD)
    scores = (
        jnp.einsum("rtkgd,rpkd->rkgtp", queries, grid_keys, preferred_element_type=jnp.float32)
        * score_scale
    )
    key_spots = seq_index * positions + jnp.arange(positions, dtype=jnp.int32)
    live_mask = (key_spots[None, :] < my_lengths[:, None])[:, None, None, None, :]
    scores = jnp.where(live_mask, scores, MASKED)
    row_peak = jnp.max(scores, axis=-1)
    weights = jnp.where(live_mask, jnp.exp(scores - row_peak[..., None]), 0.0)
    row_mass = jnp.sum(weights, axis=-1)
    gathered_sum = jnp.einsum(
        "rkgtp,rpkd->rkgtd",
        weights.astype(jnp.bfloat16),
        grid_values,
        preferred_element_type=jnp.float32,
    )
    global_peak = lax.pmax(row_peak, "seq")
    rescale = jnp.exp(row_peak - global_peak)
    row_mass, gathered_sum = (
        lax.psum((row_mass * rescale).astype(jnp.bfloat16), "seq").astype(jnp.float32),
        lax.psum((gathered_sum * rescale[..., None]).astype(jnp.bfloat16), "seq").astype(
            jnp.float32
        ),
    )
    row_peak = global_peak
    own_scores = (
        jnp.einsum("rtkgd,rskd->rkgts", queries, fresh_keys, preferred_element_type=jnp.float32)
        * score_scale
    )
    causal = new_index[None, :] <= new_index[:, None]
    own_scores = jnp.where(causal, own_scores, MASKED)
    final_peak = jnp.maximum(row_peak, jnp.max(own_scores, axis=-1))
    carried = jnp.exp(row_peak - final_peak)
    own_weights = jnp.where(causal, jnp.exp(own_scores - final_peak[..., None]), 0.0)
    row_mass = row_mass * carried + jnp.sum(own_weights, axis=-1)
    gathered_sum = gathered_sum * carried[..., None] + jnp.einsum(
        "rkgts,rskd->rkgtd",
        own_weights.astype(jnp.bfloat16),
        fresh_values,
        preferred_element_type=jnp.float32,
    )
    attended = (
        jnp.transpose(gathered_sum / row_mass[..., None], (0, 3, 1, 2, 4))
        .reshape(local_reqs, new_count, KVH * groups * HD)
        .astype(jnp.bfloat16)
    )
    headed = lax.all_to_all(attended, "req", split_axis=2, concat_axis=0, tiled=True)
    row_count = lax.axis_size("req") * local_reqs
    projected_out = lax.psum_scatter(
        jnp.dot(
            headed.reshape(row_count * new_count, -1), w_out, preferred_element_type=jnp.float32
        )
        .reshape(row_count, new_count, model_width)
        .astype(jnp.bfloat16),
        "req",
        scatter_dimension=0,
        tiled=True,
    ).astype(jnp.float32)
    out_hidden = (tokens_wide + projected_out).astype(jnp.bfloat16)
    new_hits = key_spots[None, :, None] == my_lengths[:, None, None] + new_index[None, None, :]
    filler = new_hits.astype(jnp.bfloat16)
    placed_keys = jnp.einsum(
        "rpt,rtc->rpc",
        filler,
        fresh_keys.reshape(local_reqs, new_count, kv_width),
        preferred_element_type=jnp.float32,
    ).astype(jnp.bfloat16)
    placed_values = jnp.einsum(
        "rpt,rtc->rpc",
        filler,
        fresh_values.reshape(local_reqs, new_count, kv_width),
        preferred_element_type=jnp.float32,
    ).astype(jnp.bfloat16)
    touched = jnp.any(new_hits, axis=-1)[..., None]
    keys_out = jnp.where(touched, placed_keys, cache_keys)
    values_out = jnp.where(touched, placed_values, cache_values)
    return (out_hidden, keys_out, values_out)


def solution(mesh):
    return jax.shard_map(
        shards,
        mesh=mesh,
        in_specs=(
            P("req", None, None),
            P(),
            P(None, "req"),
            P(None, "req"),
            P(None, "req"),
            P("req", None),
            P(("req", "seq"), None, None),
            P(("req", "seq"), None, None),
            P(),
            P(),
            P(),
        ),
        out_specs=(P("req", None, None), P("req", "seq", None), P("req", "seq", None)),
        check_vma=False,
    )
```

profile of v0, /device:TPU:0, one launch (start us, length us, event | category | flops | bytes accessed | tf_op | source)
XLA Modules:
  0.0 471.1 jit_solution(13504681853313874680)
XLA Ops:
  7.2 0.8 fusion.56
  8.0 0.7 scatter_custom_fusion
  8.7 1.4 gather_fusion
  10.1 1.1 fusion.28
  11.2 1.0 fusion.30
  12.3 11.5 %all_gather.3 = bf16[32,4,2048]{2,0,1:T(8,128)(2,1)S(1)} all-gather(bf16[8,4,2048]{2,0,1:T(8,128)(2,1)S(1)} %fusion.30), channel_id=1, replica_groups=mesh['req'=4,'seq'=8] {'req'}, dimensions={0}, use_global_device_ids=true | all-gather | bytes 655360 | tf_op jit(solution)/shard_map/all_gather | solution.py:101
  23.8 3.9 copy.186
  27.7 2.3 copy.187
  29.9 2.5 fusion.26
  32.5 1.7 fusion.24
  34.2 0.3 multiply_cosine_fusion
  34.5 0.2 subtract_convert_fusion
  34.7 0.1 subtract_convert_fusion.1
  34.8 0.3 convolution_convert_fusion.1
  35.1 0.1 copy_bitcast_fusion.1
  35.3 0.9 copy.145
  36.2 3.4 all-to-all-start.1
  39.8 15.5 %scatter_custom_fusion.1 = s32[4096]{0:T(1024)S(1)} fusion(s32[4096]{0:T(1024)S(1)} %bitcast.134, s32[4096]{0:T(1024)S(1)} %get-tuple-element.47, s32[]{:T(128)} %constant.90.clone.1), kind=kCustom, calls=%fused_computation.83 | custom fusion | bytes 16388 | tf_op jit(solution)/shard_map/scatter | solution.py:78
  55.4 2.5 sort.45
  58.0 5.0 %gather_fusion.1 = bf16[128,16,1024]{2,1,0:T(8,128)(2,1)} fusion(bf16[128,16,1024]{2,1,0:T(8,128)(2,1)} %param.17, s32[1024]{0:T(1024)S(1)} %pad_clamp_fusion.1), kind=kCustom, calls=%fused_computation.1 | custom fusion | bytes 8389120 | tf_op jit(solution)/shard_map/gather | solution.py:90
  63.0 5.0 %gather_fusion.2 = bf16[128,16,1024]{2,1,0:T(8,128)(2,1)} fusion(bf16[128,16,1024]{2,1,0:T(8,128)(2,1)} %param.18, s32[1024]{0:T(1024)S(1)} %pad_clamp_fusion.1), kind=kCustom, calls=%fused_computation.2 | custom fusion | bytes 8389120 | tf_op jit(solution)/shard_map/gather | solution.py:90
  68.0 7.5 %pad_maximum_fusion = bf16[32,4,2,16,1024]{4,3,2,1,0:T(8,128)(2,1)} fusion(bf16[32,4,1,16,1024]{4,3,2,1,0:T(8,128)(2,1)} %bitcast.120, bf16[32,4,1,16,1024]{4,3,2,1,0:T(8,128)(2,1)} %bitcast.119), kind=kLoop, calls=%fused_computation.7 | loop fusion | flops 4194304 | bytes 16777216 | tf_op jit(solution)/shard_map/stack | solution.py:90
  75.5 6.4 %all-to-all-start = ((bf16[32,4,2,16,1024]{4,3,2,1,0:T(8,128)(2,1)}), bf16[32,4,2,16,1024]{4,3,2,1,0:T(8,128)(2,1)}, u32[]{:S(2)}, u32[]{:S(2)}) async-start(bf16[32,4,2,16,1024]{4,3,2,1,0:T(8,128)(2,1)} %pad_maximum_fusion), calls=%async_computation | async-start | bytes 16777216 | tf_op jit(solution)/shard_map/all_to_all | solution.py:92
  82.0 15.7 %scatter_custom_fusion.2 = s32[4096]{0:T(1024)S(1)} fusion(s32[4096]{0:T(1024)S(1)} %bitcast.135, s32[4096]{0:T(1024)S(1)} %bitcast.133, s32[]{:T(128)} %constant.90.clone.1), kind=kCustom, calls=%fused_computation.81 | custom fusion | bytes 16388 | tf_op jit(solution)/shard_map/scatter | solution.py:81
  97.8 2.5 sort.46
  100.4 2.5 sort.47
  102.9 0.6 dynamic-slice
  104.7 0.3 fusion.39
  105.0 0.5 copy.159
  105.6 161.2 %all-to-all-done = bf16[32,4,2,16,1024]{4,3,2,1,0:T(8,128)(2,1)} async-done(((bf16[32,4,2,16,1024]{4,3,2,1,0:T(8,128)(2,1)}), bf16[32,4,2,16,1024]{4,3,2,1,0:T(8,128)(2,1)}, u32[]{:S(2)}, u32[]{:S(2)}) %all-to-all-start) | async-done | bytes 8388640 | tf_op jit(solution)/shard_map/all_to_all | solution.py:92
  266.8 9.9 %gather_fusion.3 = bf16[128,2,16,1024]{3,2,1,0:T(8,128)(2,1)} fusion(bf16[128,2,16,1024]{3,2,1,0:T(8,128)(2,1)} %bitcast.7, s32[1024]{0:T(1024)S(1)} %pad_clamp_fusion), kind=kCustom, calls=%fused_computation.3 | custom fusion | bytes 16777728 | tf_op jit(solution)/shard_map/gather | solution.py:93
  276.7 5.4 %fusion.59 = (bf16[8,16,1,16,1024]{4,3,2,1,0:T(8,128)(2,1)}, bf16[8,16,1,16,1024]{4,3,2,1,0:T(8,128)(2,1)S(1)}) fusion(bf16[8,16,2,16,1024]{4,3,2,1,0:T(8,128)(2,1)} %bitcast.116), kind=kLoop, calls=%fused_computation.119 | loop fusion | bytes 16777216 | tf_op jit(solution)/shard_map/slice | solution.py:96
  282.2 1.1 copy.208
  283.3 0.9 copy-done.1
  284.2 0.3 bitcast_bitcast_fusion.1
  284.5 1.6 fusion.61
  286.1 0.3 copy.154
  286.4 0.8 fusion.37
  287.2 0.3 copy.166
  287.4 26.0 %pmax.7 = f32[8,8,2,4]{1,0,3,2:T(8,128)S(1)} all-reduce(f32[8,8,2,4]{1,0,3,2:T(8,128)S(1)} %copy.154), channel_id=1, replica_groups=mesh['req'=4,'seq'=8] {'seq'}, use_global_device_ids=true, to_apply=%region_8.9 | all-reduce | flops 512 | bytes 4096 | tf_op jit(solution)/shard_map/pmax | solution.py:143
  313.4 0.1 fusion.35
  313.5 25.9 %psum.15 = bf16[8,8,2,4]{1,0,3,2:T(8,128)(2,1)S(1)} all-reduce(bf16[8,8,2,4]{1,0,3,2:T(8,128)(2,1)S(1)} %get-tuple-element.29), channel_id=1, replica_groups=mesh['req'=4,'seq'=8] {'seq'}, use_global_device_ids=true, to_apply=%region_12.13 | all-reduce | flops 512 | bytes 2048 | tf_op jit(solution)/shard_map/psum | solution.py:146
  339.5 0.2 copy.155
  339.6 3.3 copy.209
  342.9 0.3 bitcast_bitcast_fusion
  343.2 1.3 fusion.13
  344.6 0.2 copy.162
  344.7 0.2 copy.169
  344.9 0.5 copy.164
  345.4 50.0 %all-reduce.4.cloned.1.call-done = bf16[8,8,2,4,128]{4,3,2,1,0:T(4,128)(2,1)} async-done(((bf16[8,8,2,4,128]{4,3,2,1,0:T(4,128)(2,1)}), bf16[8,8,2,4,128]{4,3,2,1,0:T(4,128)(2,1)}) %all-reduce.4.cloned.1.call-update) | async-done | bytes 131088 | tf_op jit(solution)/shard_map/psum | solution.py:147
  395.4 1.3 fusion.16
  396.7 2.4 copy.196
  399.1 4.0 reshape.420
  403.2 3.6 all-to-all-start.2
  406.8 0.1 compare_reduce_fusion
  407.0 4.8 %all-to-all-done.2 = bf16[4,2,8192]{2,1,0:T(2,128)(2,1)S(1)} async-done(((bf16[4,2,8192]{2,1,0:T(2,128)(2,1)}), bf16[4,2,8192]{2,1,0:T(2,128)(2,1)S(1)}, u32[]{:S(2)}, u32[]{:S(2)}) %all-to-all-start.2) | async-done | bytes 131104 | tf_op jit(solution)/shard_map/all_to_all | solution.py:173
  411.8 3.4 reshape.421
  415.3 2.8 copy.173
  418.1 1.3 convolution_convert_fusion
  419.4 5.3 %bitcast_select_fusion = bf16[8,256,1024]{2,1,0:T(8,128)(2,1)} fusion(bf16[8,16,1,16,1024]{4,3,2,1,0:T(8,128)(2,1)} %get-tuple-element.31, pred[8,256]{1,0:T(8,128)(4,1)S(1)} %compare_reduce_fusion, bf16[8,4,1024]{2,1,0:T(4,128)(2,1)S(1)} %reshape_reshape.7, s32[8,4]{1,0:T(8,128)S(1)} %iota_add_fusion, s32[256]{0:T(256)S(1)} %iota_add_fusion.1), kind=kOutput, calls=%fused_computation.10 | convolution fusion | flops 20979712 | bytes 8457344 | tf_op jit(solution)/shard_map/rpt,rtc->rpc/dot_general | solution.py:194
  424.7 3.9 bitcast_select_fusion.1
  428.6 33.8 %all-reduce.6.cloned.1.call-done = bf16[32,4,2048]{2,0,1:T(8,128)(2,1)} async-done(((bf16[32,4,2048]{2,0,1:T(8,128)(2,1)}), bf16[32,4,2048]{2,0,1:T(8,128)(2,1)}) %all-reduce.6.cloned.1.call-update) | async-done | bytes 524304
  462.5 1.0 fusion.31
  463.5 0.8 copy.176
  (58 shorter events, 1.4 us)
Async XLA Ops:
  7.2 410.9 %copy-start = (bf16[512,2048]{1,0:T(8,128)(2,1)S(1)}, bf16[512,2048]{1,0:T(8,128)(2,1)}, u32[]{:S(2)}) copy-start(bf16[512,2048]{1,0:T(8,128)(2,1)} %param.16) | copy-start | bytes 6291460
  29.9 4.8 %copy-start.4 = (bf16[2048,256]{1,0:T(8,128)(2,1)S(1)}, bf16[2048,256]{1,0:T(8,128)(2,1)}, u32[]{:S(2)}) copy-start(bf16[2048,256]{1,0:T(8,128)(2,1)} %param.15) | copy-start | bytes 3145732
  32.4 7.2 %copy-start.5 = (s32[32,128]{1,0:T(8,128)S(1)}, s32[32,128]{1,0:T(8,128)}, u32[]{:S(2)}) copy-start(s32[32,128]{1,0:T(8,128)} %param.21) | copy-start | bytes 49156
  36.2 39.2 %all-to-all-start.1 = ((bf16[32,4,1024]{2,1,0:T(4,128)(2,1)}), bf16[32,4,1024]{2,1,0:T(4,128)(2,1)S(1)}, u32[]{:S(2)}, u32[]{:S(2)}) async-start(bf16[32,4,1024]{2,1,0:T(4,128)(2,1)} %copy.145), calls=%async_computation.1 | async-start | bytes 524288 | tf_op jit(solution)/shard_map/all_to_all | solution.py:117
  75.5 27.5 %copy-start.6 = (u32[32]{0:T(128)S(1)}, u32[32]{0:T(128)}, u32[]{:S(2)}) copy-start(u32[32]{0:T(128)} %constant.115) | copy-start | bytes 388
  75.5 191.3 %all-to-all-start = ((bf16[32,4,2,16,1024]{4,3,2,1,0:T(8,128)(2,1)}), bf16[32,4,2,16,1024]{4,3,2,1,0:T(8,128)(2,1)}, u32[]{:S(2)}, u32[]{:S(2)}) async-start(bf16[32,4,2,16,1024]{4,3,2,1,0:T(8,128)(2,1)} %pad_maximum_fusion), calls=%async_computation | async-start | bytes 16777216 | tf_op jit(solution)/shard_map/all_to_all | solution.py:92
  81.9 313.5 %all-reduce.4.cloned.1.call-start = ((), (), s32[]{:S(2)}) async-start(), calls=%async_computation.3 | async-start | bytes 262144 | tf_op jit(solution)/shard_map/psum | solution.py:147
  282.2 2.1 copy-start.1
  403.2 8.7 %all-to-all-start.2 = ((bf16[4,2,8192]{2,1,0:T(2,128)(2,1)}), bf16[4,2,8192]{2,1,0:T(2,128)(2,1)S(1)}, u32[]{:S(2)}, u32[]{:S(2)}) async-start(bf16[4,2,8192]{2,1,0:T(2,128)(2,1)} %reshape.420), calls=%async_computation.2 | async-start | bytes 262144 | tf_op jit(solution)/shard_map/all_to_all | solution.py:173
  406.8 55.7 %all-reduce.6.cloned.1.call-start = ((), (), s32[]{:S(2)}) async-start(), calls=%async_computation.4 | async-start | bytes 1048576
  419.4 5.3 %copy-start.2 = (bf16[8,16,1,16,1024]{4,3,2,1,0:T(8,128)(2,1)S(1)}, bf16[8,16,1,16,1024]{4,3,2,1,0:T(8,128)(2,1)}, u32[]{:S(2)}) copy-start(bf16[8,16,1,16,1024]{4,3,2,1,0:T(8,128)(2,1)} %copy-done.1) | copy-start | bytes 12582916
  424.7 37.7 %copy-start.3 = (bf16[8,4,2048]{2,1,0:T(4,128)(2,1)S(1)}, bf16[8,4,2048]{2,1,0:T(4,128)(2,1)}, u32[]{:S(2)}) copy-start(bf16[8,4,2048]{2,1,0:T(4,128)(2,1)} %param.11) | copy-start | bytes 393220
Sparse Core Ops, SparseCore 0:
  344.7 50.7 all-reduce.3
  419.5 42.8 all-reduce.5
where the time goes:
time: 472 us; the launch traced here: 471 us
  waiting for transfers between devices  250 us (53%)
  local copies, waits for them, and re-layouts  88.3 us (19%)
  blocking collectives  63.4 us (13%)
  other arithmetic  21.4 us (5%)
  matrix products  19.5 us (4%)
  between operations  15.1 us (3%)
  starting transfers between devices  13.5 us (3%)
    all_to_all x1, waiting for transfers between devices, shards(): lax.all_to_all(outgoing, ('req', 'seq'), split_axis=0, concat_axis=0, til...  161 us
    psum x1, waiting for transfers between devices, shards(): lax.psum((gathered_sum * rescale[..., None]).astype(jnp.bfloat16), 'seq')  50 us
    unnamed x3, waiting for transfers between devices  33.9 us
    pmax x1, blocking collectives, shards(): global_peak = lax.pmax(row_peak, 'seq')  26 us
    psum x1, blocking collectives, shards(): lax.psum((row_mass * rescale).astype(jnp.bfloat16), 'seq')  25.9 us
    scatter x1, local copies, waits for them, and re-layouts, shards(): jnp.zeros((pool_total,), jnp.int32).at[home_index.reshape(-1)]  15.7 us
    scatter x1, local copies, waits for them, and re-layouts, shards(): jnp.zeros((pool_total,), jnp.int32).at[page_table.reshape(-1)]  15.5 us
    unnamed x20, local copies, waits for them, and re-layouts  14.2 us
  transfers between devices with their start and end apart: 5, of which 4 were waited for; matrix products, arithmetic and copies ran while one was open for 15% of the time, Pallas kernels for 0%

commit v1 on v0

v1 whole, which is shorter than its diff:
```python
import functools
import math

import jax
import jax.numpy as jnp
from jax import lax
from jax.experimental import pallas as pl
from jax.experimental.pallas import tpu as pltpu
from jax.sharding import PartitionSpec as P

H = 16
KVH = 8
HD = 128
GROUPS = H // KVH

NORM_EPS = 1e-05
ROPE_BASE = 1000000.0
MASKED = -1e30
VMEM_BYTES = 48 * 1024 * 1024


def rotate(values, places):
    half_dim = values.shape[-1] // 2
    steps_up = jnp.arange(half_dim, dtype=jnp.float32) * (2.0 / values.shape[-1])
    inverse = ROPE_BASE ** (-steps_up)
    angles = places.astype(jnp.float32)[..., None] * inverse
    cosine = jnp.cos(angles)[..., None, :]
    sine_part = jnp.sin(angles)[..., None, :]
    first_half = values[..., :half_dim]
    second_half = values[..., half_dim:]
    return jnp.concatenate(
        [
            first_half * cosine - second_half * sine_part,
            second_half * cosine + first_half * sine_part,
        ],
        axis=-1,
    )


def attend_kernel(
    new_count, page_info, own_info, q_ref, k_ref, v_ref, kn_ref, vn_ref, acc_ref, max_ref, sum_ref
):
    scale = 1.0 / math.sqrt(HD)
    q = q_ref[0]
    rows = q.shape[0]
    dims = (((1,), (1,)), ((), ()))
    scores = lax.dot_general(q, k_ref[...], dims, preferred_element_type=jnp.float32) * scale
    own = lax.dot_general(q, kn_ref[0], dims, preferred_element_type=jnp.float32) * scale
    row_ids = lax.broadcasted_iota(jnp.int32, (rows, 1), 0)
    row_slot = row_ids // (GROUPS * new_count)
    row_token = row_ids % new_count
    live = page_info[...] == row_slot
    own_token = lax.broadcasted_iota(jnp.int32, own.shape, 1) % new_count
    own_live = (own_info[...] == row_slot) & (own_token <= row_token)
    scores = jnp.where(live, scores, MASKED)
    own = jnp.where(own_live, own, MASKED)
    peak = jnp.maximum(
        jnp.max(scores, axis=-1, keepdims=True), jnp.max(own, axis=-1, keepdims=True)
    )
    weights = jnp.where(live, jnp.exp(scores - peak), 0.0)
    own_weights = jnp.where(own_live, jnp.exp(own - peak), 0.0)
    mass = jnp.sum(weights, axis=-1, keepdims=True) + jnp.sum(own_weights, axis=-1, keepdims=True)
    acc_ref[0] = jnp.dot(
        weights.astype(jnp.bfloat16), v_ref[...], preferred_element_type=jnp.float32
    ) + jnp.dot(own_weights.astype(jnp.bfloat16), vn_ref[0], preferred_element_type=jnp.float32)
    max_ref[0] = peak
    sum_ref[0] = mass


def attend(page_info, own_info, queries, keys, values, keys_new, values_new, new_count):
    rows = queries.shape[1]
    spots = keys.shape[0]
    own = keys_new.shape[1]
    whole = lambda shape: pl.BlockSpec(shape, lambda h: (0, 0))
    per_head = lambda shape: pl.BlockSpec((1,) + shape, lambda h: (h, 0, 0))
    return pl.pallas_call(
        functools.partial(attend_kernel, new_count),
        grid=(KVH,),
        in_specs=[
            whole((1, spots)),
            whole((1, own)),
            per_head((rows, HD)),
            pl.BlockSpec((spots, HD), lambda h: (0, h)),
            pl.BlockSpec((spots, HD), lambda h: (0, h)),
            per_head((own, HD)),
            per_head((own, HD)),
        ],
        out_specs=[per_head((rows, HD)), per_head((rows, 1)), per_head((rows, 1))],
        out_shape=[
            jax.ShapeDtypeStruct((KVH, rows, HD), jnp.float32),
            jax.ShapeDtypeStruct((KVH, rows, 1), jnp.float32),
            jax.ShapeDtypeStruct((KVH, rows, 1), jnp.float32),
        ],
        compiler_params=pltpu.CompilerParams(vmem_limit_bytes=VMEM_BYTES),
        cost_estimate=pl.CostEstimate(
            flops=4 * KVH * rows * spots * HD,
            bytes_accessed=4 * KVH * spots * HD,
            transcendentals=KVH * rows * spots,
        ),
        name="attend_held_pages",
    )(page_info, own_info, queries, keys, values, keys_new, values_new)


def place_kernel(placement, starts, fresh, incoming, out, buf, in_sems, out_sems):
    slots, new_count, _ = fresh.shape
    pages, page_len, _ = buf.shape
    per_slot = pages // slots
    for slot in range(slots):
        for step in range(per_slot):
            page = slot * per_slot + step
            pltpu.make_async_copy(
                incoming.at[placement[page]], buf.at[page], in_sems.at[slot]
            ).start()
    for slot in range(slots):
        mine = pl.ds(slot * per_slot, per_slot)
        pltpu.make_async_copy(incoming.at[mine], buf.at[mine], in_sems.at[slot]).wait()
        for token in range(new_count):
            spot = starts[slot] + token

            @pl.when((spot >= 0) & (spot < per_slot * page_len))
            def _():
                page = slot * per_slot + spot // page_len
                block = buf[page].astype(jnp.float32)
                here = lax.broadcasted_iota(jnp.int32, block.shape, 0) == spot % page_len
                row = fresh[slot, pl.ds(token, 1), :]
                buf[page] = jnp.where(here, row, block).astype(buf.dtype)

        pltpu.make_async_copy(buf.at[mine], out.at[mine], out_sems.at[slot]).start()
    for slot in range(slots):
        mine = pl.ds(slot * per_slot, per_slot)
        pltpu.make_async_copy(buf.at[mine], out.at[mine], out_sems.at[slot]).wait()


def place(placement, starts, fresh, incoming, name):
    slots = fresh.shape[0]
    smem = pl.BlockSpec(memory_space=pltpu.SMEM)
    return pl.pallas_call(
        place_kernel,
        in_specs=[
            smem,
            smem,
            pl.BlockSpec(memory_space=pltpu.VMEM),
            pl.BlockSpec(memory_space=pl.ANY),
        ],
        out_specs=pl.BlockSpec(memory_space=pl.ANY),
        out_shape=jax.ShapeDtypeStruct(incoming.shape, incoming.dtype),
        scratch_shapes=[
            pltpu.VMEM(incoming.shape, incoming.dtype),
            pltpu.SemaphoreType.DMA((slots,)),
            pltpu.SemaphoreType.DMA((slots,)),
        ],
        compiler_params=pltpu.CompilerParams(vmem_limit_bytes=VMEM_BYTES),
        cost_estimate=pl.CostEstimate(
            flops=0, bytes_accessed=2 * incoming.size * 2, transcendentals=0
        ),
        name=name,
    )(placement, starts, fresh, incoming)


def shards(
    new_tokens,
    norm_gain,
    w_query,
    w_key,
    w_value,
    w_out,
    pool_keys,
    pool_values,
    cache_lengths,
    owner,
    page_table,
):
    req_count = lax.axis_size("req")
    seq_count = lax.axis_size("seq")
    devices = req_count * seq_count
    req_index = lax.axis_index("req")
    seq_index = lax.axis_index("seq")
    device_index = req_index * seq_count + seq_index
    local_reqs, new_count, model_width = new_tokens.shape
    slot_total = owner.shape[0]
    pages_dev, page_len, kv_width = pool_keys.shape
    pages_req = page_table.shape[1]
    pages_home = pages_req // seq_count
    positions = pages_home * page_len
    per_peer = pages_dev // devices
    query_cols = w_query.shape[1]
    key_cols = w_key.shape[1]
    i32 = jnp.int32
    local_pages = jnp.arange(pages_dev, dtype=i32)

    logical = jnp.arange(pages_req, dtype=i32)[None, :]
    home_index = (
        (owner[:, None] // local_reqs * seq_count + logical // pages_home) * pages_dev
        + owner[:, None] % local_reqs * pages_home
        + logical % pages_home
    )
    held = page_table[None] == (device_index * pages_dev + local_pages)[:, None, None]
    held_homes = jnp.sum(jnp.where(held, home_index[None], 0), axis=(1, 2))
    send_rank = jnp.sum((held_homes[None, :] < held_homes[:, None]).astype(i32), axis=1)
    send_order = jnp.sum(
        jnp.where(send_rank[None, :] == local_pages[:, None], local_pages[None, :], 0), axis=1
    )

    def move(pool):
        outgoing = pool.at[send_order].get(mode="promise_in_bounds")
        outgoing = outgoing.reshape(devices, per_peer, page_len, kv_width)
        incoming = lax.all_to_all(outgoing, ("req", "seq"), split_axis=0, concat_axis=0, tiled=True)
        return incoming.reshape(pages_dev, page_len, kv_width)

    in_keys = move(pool_keys)
    in_values = move(pool_values)

    slots = jnp.arange(slot_total, dtype=i32)
    slot_owned = owner[None, :] == slots[:, None]
    slot_request = jnp.sum(jnp.where(slot_owned, slots[None, :], 0), axis=1)
    slot_lengths = jnp.sum(jnp.where(slot_owned, cache_lengths[None, :], 0), axis=1)
    my_requests = lax.dynamic_slice_in_dim(slot_request, req_index * local_reqs, local_reqs)
    my_lengths = lax.dynamic_slice_in_dim(slot_lengths, req_index * local_reqs, local_reqs)
    seq_pages = lax.dynamic_slice_in_dim(page_table, seq_index * pages_home, pages_home, axis=1)
    is_mine = my_requests[:, None, None] == slots[None, :, None]
    source = jnp.sum(jnp.where(is_mine, seq_pages[None], 0), axis=1).reshape(-1) // pages_dev
    ahead = (source[None, :] == source[:, None]) & (local_pages[None, :] < local_pages[:, None])
    placement = source * per_peer + jnp.sum(ahead.astype(i32), axis=1)

    tokens_wide = new_tokens.astype(jnp.float32)
    square_mean = jnp.mean(tokens_wide * tokens_wide, axis=-1, keepdims=True)
    normed = (tokens_wide * lax.rsqrt(square_mean + NORM_EPS) * norm_gain).astype(jnp.bfloat16)
    flat_rows = lax.all_gather(
        normed.reshape(local_reqs * new_count, model_width), "req", axis=0, tiled=True
    )
    new_index = jnp.arange(new_count, dtype=i32)
    places = slot_lengths[:, None] + new_index[None, :]
    heads = lambda w: jnp.dot(flat_rows, w, preferred_element_type=jnp.float32)
    queries_now = heads(w_query).reshape(slot_total, new_count, query_cols // HD, HD)
    keys_now = heads(w_key).reshape(slot_total, new_count, key_cols // HD, HD)
    queries_now = rotate(queries_now, places).reshape(slot_total * new_count, query_cols)
    keys_now = rotate(keys_now, places).reshape(slot_total * new_count, key_cols)
    projected = jnp.concatenate([queries_now, keys_now, heads(w_value)], axis=-1)
    every = lax.all_gather(projected.astype(jnp.bfloat16), "req", axis=0, tiled=False)
    own_kv = key_cols // HD
    queries = every[..., :query_cols].reshape(
        req_count, slot_total, new_count, own_kv, GROUPS, HD
    )
    queries = jnp.transpose(queries, (0, 3, 1, 4, 2, 5)).reshape(KVH, -1, HD)

    def by_head(part):
        part = part.reshape(req_count, slot_total * new_count, own_kv, HD)
        return jnp.transpose(part, (0, 2, 1, 3)).reshape(KVH, slot_total * new_count, HD)

    def of_mine(part):
        part = part.reshape(req_count, slot_total, new_count, key_cols)
        part = lax.dynamic_slice_in_dim(part, req_index * local_reqs, local_reqs, axis=1)
        part = jnp.transpose(part, (1, 2, 0, 3)).reshape(local_reqs, new_count, kv_width)
        return part.astype(jnp.float32)

    new_keys = every[..., query_cols : query_cols + key_cols]
    new_values = every[..., query_cols + key_cols :]

    held_dev = held_homes // pages_dev
    held_slot = held_dev // seq_count * local_reqs + held_homes % pages_dev // pages_home
    held_first = (held_dev % seq_count * pages_home + held_homes % pages_home) * page_len
    held_length = jnp.sum(
        jnp.where(held_slot[:, None] == slots[None, :], slot_lengths[None, :], 0), axis=1
    )
    spots = held_first[:, None] + jnp.arange(page_len, dtype=i32)[None, :]
    page_info = jnp.where(spots < held_length[:, None], held_slot[:, None], -1).reshape(1, -1)
    own_info = jnp.where(device_index == 0, jnp.repeat(slots, new_count), -1).reshape(1, -1)
    total, peak, mass = attend(
        page_info,
        own_info,
        queries,
        pool_keys.reshape(pages_dev * page_len, kv_width),
        pool_values.reshape(pages_dev * page_len, kv_width),
        by_head(new_keys),
        by_head(new_values),
        new_count,
    )
    peak = peak[..., 0]
    mass = mass[..., 0]
    rows = peak.shape[1]
    rescale = jnp.exp(peak - lax.pmax(peak, ("req", "seq")))
    packed = jnp.concatenate(
        [total * rescale[..., None], (mass * rescale).reshape(KVH, rows // HD, HD)], axis=1
    ).astype(jnp.bfloat16)
    packed = lax.psum(packed, ("req", "seq"))
    packed = lax.dynamic_slice_in_dim(packed, req_index * own_kv, own_kv).astype(jnp.float32)
    attended = packed[:, :rows] / packed[:, rows:].reshape(own_kv, rows, 1)
    attended = attended.reshape(own_kv, slot_total, GROUPS, new_count, HD)
    attended = (
        jnp.transpose(attended, (1, 3, 0, 2, 4))
        .reshape(slot_total * new_count, query_cols)
        .astype(jnp.bfloat16)
    )
    shares = jnp.dot(attended, w_out, preferred_element_type=jnp.float32).astype(jnp.bfloat16)
    summed = lax.psum_scatter(shares, "req", scatter_dimension=0, tiled=True).astype(jnp.float32)
    out_hidden = (tokens_wide + summed.reshape(tokens_wide.shape)).astype(jnp.bfloat16)

    starts = my_lengths - seq_index * positions
    out_shape = (local_reqs, positions, kv_width)
    keys_out = place(placement, starts, of_mine(new_keys), in_keys, "place_keys")
    values_out = place(placement, starts, of_mine(new_values), in_values, "place_values")
    return (out_hidden, keys_out.reshape(out_shape), values_out.reshape(out_shape))


def solution(mesh):
    return jax.shard_map(
        shards,
        mesh=mesh,
        in_specs=(
            P("req", None, None),
            P(),
            P(None, "req"),
            P(None, "req"),
            P(None, "req"),
            P("req", None),
            P(("req", "seq"), None, None),
            P(("req", "seq"), None, None),
            P(),
            P(),
            P(),
        ),
        out_specs=(P("req", None, None), P("req", "seq", None), P("req", "seq", None)),
        check_vma=False,
    )
```

time: 472 us -> 442 us (0.936)
  local copies, waits for them, and re-layouts: 88.3 us -> 17.3 us
  waiting for transfers between devices: 250 us -> 278 us
  Pallas kernels: 0 us -> 21.8 us
  blocking collectives: 63.4 us -> 77.8 us
  matrix products: 19.5 us -> 6.38 us
  other arithmetic: 21.4 us -> 14.2 us
    all_to_all x3 -> x2, waiting for transfers between devices: 166 us -> 89.8 us  [move(): lax.all_to_all(outgoing, ('req', 'seq'), split_axis=0, concat_axis=0, til...]
    psum x1, waiting for transfers between devices: 50 us -> 126 us  [shards(): packed = lax.psum(packed, ('req', 'seq'))]
    all_gather x0 -> x1, waiting for transfers between devices: none -> 36.6 us  [shards(): lax.all_gather(projected.astype(jnp.bfloat16), 'req', axis=0, tiled=False)]
    unnamed x3, waiting for transfers between devices: 33.9 us -> 0.05 us
    scatter x3 -> x0, local copies, waits for them, and re-layouts: 31.9 us -> none  [the longest x1 15.7 us: shards(): jnp.zeros((pool_total,), jnp.int32).at[home_index.reshape(-1)]]
    psum x1 -> x0, blocking collectives: 25.9 us -> none  [shards(): lax.psum((row_mass * rescale).astype(jnp.bfloat16), 'seq')]
    reduce_scatter x0 -> x1, waiting for transfers between devices: none -> 25.8 us  [shards(): lax.psum_scatter(shares, 'req', scatter_dimension=0, tiled=True)]
    all_gather x1, blocking collectives: 11.5 us -> 37 us  [shards(): lax.all_gather(normed.reshape(local_reqs * new_count, model_width), 'req'...]
  transfers between devices with their start and end apart: 5 -> 5, of which waited for: 4 -> 4; matrix products, arithmetic and copies ran while one was open for 15% -> 6% of each run, Pallas kernels for 0% -> 4%
where the time goes in v1:
time: 442 us; the launch traced here: 441 us
  waiting for transfers between devices  278 us (63%)
  blocking collectives  77.8 us (18%)
  Pallas kernels  21.8 us (5%)
  local copies, waits for them, and re-layouts  17.3 us (4%)
  between operations  14.3 us (3%)
  other arithmetic  14.2 us (3%)
  starting transfers between devices  11.4 us (3%)
  matrix products  6.38 us (1%)
    psum x1, waiting for transfers between devices, shards(): packed = lax.psum(packed, ('req', 'seq'))  126 us
    all_to_all x2, waiting for transfers between devices, move(): lax.all_to_all(outgoing, ('req', 'seq'), split_axis=0, concat_axis=0, til...  89.8 us
    pmax x1, blocking collectives, shards(): rescale = jnp.exp(peak - lax.pmax(peak, ('req', 'seq')))  40.8 us
    all_gather x1, blocking collectives, shards(): lax.all_gather(normed.reshape(local_reqs * new_count, model_width), 'req'...  37 us
    all_gather x1, waiting for transfers between devices, shards(): lax.all_gather(projected.astype(jnp.bfloat16), 'req', axis=0, tiled=False)  36.6 us
    reduce_scatter x1, waiting for transfers between devices, shards(): lax.psum_scatter(shares, 'req', scatter_dimension=0, tiled=True)  25.8 us
    pallas_call x1, Pallas kernels, attend(): pl.pallas_call(functools.partial(attend_kernel, new_count), grid=(KVH,),...  13.1 us
    all_to_all x2, starting transfers between devices, move(): lax.all_to_all(outgoing, ('req', 'seq'), split_axis=0, concat_axis=0, til...  11.1 us
  transfers between devices with their start and end apart: 5, of which 4 were waited for; matrix products, arithmetic and copies ran while one was open for 6% of the time, Pallas kernels for 4%

profile of v1, /device:TPU:0, one launch (start us, length us, event | category | flops | bytes accessed | tf_op | source)
XLA Modules:
  0.0 441.5 jit_solution(9752553114157120382)
XLA Ops:
  7.2 0.8 fusion.14
  8.0 0.1 add_add_fusion
  8.1 3.3 select_reduce_fusion
  11.4 0.2 convert_reduce_fusion
  11.6 0.1 select_reduce_fusion.1
  11.7 5.0 %gather_fusion.1 = bf16[128,16,1024]{2,1,0:T(8,128)(2,1)} fusion(bf16[128,16,1024]{2,1,0:T(8,128)(2,1)} %param.18, s32[1024]{0:T(1024)S(1)} %pad_clamp_fusion), kind=kCustom, calls=%fused_computation.1 | custom fusion | bytes 8389120 | tf_op jit(solution)/shard_map/gather | solution.py:205
  16.7 7.4 %all-to-all-start.1 = ((bf16[32,4,16,1024]{3,2,1,0:T(8,128)(2,1)}), bf16[32,4,16,1024]{3,2,1,0:T(8,128)(2,1)}, u32[]{:S(2)}, u32[]{:S(2)}) async-start(bf16[32,4,16,1024]{3,2,1,0:T(8,128)(2,1)} %bitcast.48), calls=%async_computation.2 | async-start | bytes 8388608 | tf_op jit(solution)/shard_map/all_to_all | solution.py:207
  24.2 5.1 %gather_fusion = bf16[128,16,1024]{2,1,0:T(8,128)(2,1)} fusion(bf16[128,16,1024]{2,1,0:T(8,128)(2,1)} %param.17, s32[1024]{0:T(1024)S(1)} %pad_clamp_fusion), kind=kCustom, calls=%fused_computation | custom fusion | bytes 8389120 | tf_op jit(solution)/shard_map/gather | solution.py:205
  29.2 0.2 fusion.1
  29.4 89.8 %all-to-all-done.1 = bf16[32,4,16,1024]{3,2,1,0:T(8,128)(2,1)} async-done(((bf16[32,4,16,1024]{3,2,1,0:T(8,128)(2,1)}), bf16[32,4,16,1024]{3,2,1,0:T(8,128)(2,1)}, u32[]{:S(2)}, u32[]{:S(2)}) %all-to-all-start.1) | async-done | bytes 4194336 | tf_op jit(solution)/shard_map/all_to_all | solution.py:207
  119.2 3.7 all-to-all-start
  123.0 0.1 fusion.3
  123.2 37.0 %all_gather.7 = bf16[128,2048]{1,0:T(8,128)(2,1)S(1)} all-gather(bf16[32,2048]{1,0:T(8,128)(2,1)S(1)} %reshape.565), channel_id=1, replica_groups=mesh['req'=4,'seq'=8] {'req'}, dimensions={0}, use_global_device_ids=true | all-gather | bytes 655360 | tf_op jit(solution)/shard_map/all_gather | solution.py:228
  160.2 2.0 fusion.17
  162.3 0.1 reshape.566
  162.4 1.5 fusion.18
  164.0 0.1 select_reduce_fusion.3
  164.1 0.1 add_convert_fusion.2
  164.2 0.5 multiply_cosine_fusion
  164.8 0.3 subtract_convert_fusion
  165.0 0.2 pad_maximum_fusion.4
  165.3 0.3 subtract_convert_fusion.1
  165.6 0.2 pad_maximum_fusion.5
  165.8 1.5 fusion
  167.4 0.7 pad_maximum_fusion.1
  168.2 0.1 constant_dynamic-slice_fusion
  168.3 0.1 select_n.193.own_info
  168.5 0.1 select_reduce_fusion.4
  168.6 0.1 fusion.6
  168.7 0.1 select_n.190.page_info
  168.8 0.1 dynamic_slice.19
  168.9 36.6 %all-gather.2.cloned.1.call-done = bf16[4,128,1024]{2,1,0:T(8,128)(2,1)} async-done(((bf16[1,128,1024]{2,1,0:T(8,128)(2,1)}), bf16[4,128,1024]{2,1,0:T(8,128)(2,1)}) %all-gather.2.cloned.1.call-update) | async-done | bytes 1048592 | tf_op jit(solution)/shard_map/all_gather | solution.py:239
  205.5 1.1 slice.64
  206.5 0.1 reshape.568
  206.7 0.3 copy.26
  206.9 1.1 fusion.16
  208.1 13.1 %attend_held_pages.1 = (f32[8,256,128]{2,1,0:T(8,128)S(1)}, f32[8,256,1]{2,1,0:T(8,128)S(1)}, f32[8,256,1]{2,1,0:T(8,128)S(1)}) custom-call(s32[1,2048]{1,0:T(1,128)S(1)} %select_n.190.page_info, s32[1,128]{1,0:T(1,128)S(1)} %select_n.193.own_info, bf16[8,256,128]{2,1,0:T(8,128)(2,1)S(1)} %bitcast.42, bf16[2048,1024]{1,0:T(8,128)(2,1)} %bitcast.45, ...), custom_call_target="tpu_custom_call" | custom-call | flops 2147483648 | bytes 8388608 | tf_op jit(solution)/shard_map/attend_held_pages/pallas_call | solution.py:76
  221.2 1.0 copy-done.1
  222.2 1.0 copy-done.2
  223.2 1.6 reduce
  224.7 1.6 reduce.1
  226.3 40.8 %pmax.7 = f32[8,256]{1,0:T(8,128)S(1)} all-reduce(f32[8,256]{1,0:T(8,128)S(1)} %reduce), channel_id=1, replica_groups=mesh['req'=4,'seq'=8] {'req','seq'}, use_global_device_ids=true, to_apply=%region_4.5 | all-reduce | flops 2048 | bytes 16384 | tf_op jit(solution)/shard_map/pmax | solution.py:281
  267.1 0.3 multiply_convert_fusion
  267.4 0.8 pad_maximum_fusion
  268.3 0.2 reduce-scatter.2.cloned.1.call-start
  268.5 0.1 iota_compare_fusion.4
  268.6 0.2 select_reduce_fusion.2
  268.8 126.1 %all-reduce.2.cloned.1.call-done = bf16[8,258,128]{2,1,0:T(8,128)(2,1)} async-done(((bf16[8,258,128]{2,1,0:T(8,128)(2,1)}), bf16[8,258,128]{2,1,0:T(8,128)(2,1)}) %all-reduce.2.cloned.1.call-update) | async-done | bytes 528400 | tf_op jit(solution)/shard_map/psum | solution.py:285
  394.9 0.9 dynamic-slice_convert_fusion
  395.8 0.1 fusion.5
  396.0 0.1 copy.36
  396.2 1.3 convolution_convert_fusion
  397.5 0.1 dynamic-slice_subtract_fusion.starts
  397.6 0.1 reshape.577
  397.6 0.2 convert_reduce_fusion.1
  397.9 0.2 copy.32
  398.1 0.1 reshape.589.fresh
  398.2 0.2 copy.31
  398.5 0.1 reshape.588.fresh
  398.6 25.8 %reduce-scatter.2.cloned.1.call-done = bf16[32,2048]{1,0:T(8,128)(2,1)} async-done(((bf16[128,2048]{1,0:T(8,128)(2,1)}), bf16[32,2048]{1,0:T(8,128)(2,1)}) %reduce-scatter.2.cloned.1.call-update) | async-done | bytes 131088 | tf_op jit(solution)/shard_map/reduce_scatter | solution.py:295
  424.4 1.0 reshape.587
  425.4 0.7 fusion.4
  426.1 4.4 place_values.1
  430.5 4.4 place_keys.1
  (47 shorter events, 0.8 us)
Async XLA Ops:
  7.2 389.0 %copy-start = (bf16[512,2048]{1,0:T(8,128)(2,1)S(1)}, bf16[512,2048]{1,0:T(8,128)(2,1)}, u32[]{:S(2)}) copy-start(bf16[512,2048]{1,0:T(8,128)(2,1)} %param.16) | copy-start | bytes 6291460
  16.7 102.5 %all-to-all-start.1 = ((bf16[32,4,16,1024]{3,2,1,0:T(8,128)(2,1)}), bf16[32,4,16,1024]{3,2,1,0:T(8,128)(2,1)}, u32[]{:S(2)}, u32[]{:S(2)}) async-start(bf16[32,4,16,1024]{3,2,1,0:T(8,128)(2,1)} %bitcast.48), calls=%async_computation.2 | async-start | bytes 8388608 | tf_op jit(solution)/shard_map/all_to_all | solution.py:207
  24.2 5.1 %copy-start.4 = (bf16[8,4,2048]{2,1,0:T(4,128)(2,1)S(1)}, bf16[8,4,2048]{2,1,0:T(4,128)(2,1)}, u32[]{:S(2)}) copy-start(bf16[8,4,2048]{2,1,0:T(4,128)(2,1)} %param.11) | copy-start | bytes 393220
  119.2 3.8 copy-start.6
  119.2 311.3 %all-to-all-start = ((bf16[32,4,16,1024]{3,2,1,0:T(8,128)(2,1)}), bf16[32,4,16,1024]{3,2,1,0:T(8,128)(2,1)}, u32[]{:S(2)}, u32[]{:S(2)}) async-start(bf16[32,4,16,1024]{3,2,1,0:T(8,128)(2,1)} %bitcast.47), calls=%async_computation.1 | async-start | bytes 8388608 | tf_op jit(solution)/shard_map/all_to_all | solution.py:207
  122.9 41.1 %copy-start.7 = (s32[32]{0:T(128)S(1)}, s32[32]{0:T(128)}, u32[]{:S(2)}) copy-start(s32[32]{0:T(128)} %param.20) | copy-start | bytes 388
  122.9 41.1 %copy-start.8 = (s32[32]{0:T(128)S(1)}, s32[32]{0:T(128)}, u32[]{:S(2)}) copy-start(s32[32]{0:T(128)} %param.19) | copy-start | bytes 388
  123.0 82.5 %all-gather.2.cloned.1.call-start = ((), (), s32[]{:S(2)}) async-start(), calls=%async_computation.3 | async-start | bytes 1310720 | tf_op jit(solution)/shard_map/all_gather | solution.py:239
  162.3 5.9 %copy-start.5 = (s32[32,128]{1,0:T(8,128)S(1)}, s32[32,128]{1,0:T(8,128)}, u32[]{:S(2)}) copy-start(s32[32,128]{1,0:T(8,128)} %param.21) | copy-start | bytes 49156
  168.1 226.8 %all-reduce.2.cloned.1.call-start = ((), (), s32[]{:S(2)}) async-start(), calls=%async_computation.4 | async-start | bytes 1081344 | tf_op jit(solution)/shard_map/psum | solution.py:285
  221.2 1.0 copy-start.1
  222.2 1.0 copy-start.2
  267.4 130.4 %copy-start.3 = (bf16[4,128,1024]{2,1,0:T(8,128)(2,1)S(1)}, bf16[4,128,1024]{2,1,0:T(8,128)(2,1)}, u32[]{:S(2)}) copy-start(bf16[4,128,1024]{2,1,0:T(8,128)(2,1)} %all-gather.2.cloned.1.call-done) | copy-start | bytes 3145732
  268.3 156.1 %reduce-scatter.2.cloned.1.call-start = ((), (), s32[]{:S(2)}) async-start(), calls=%async_computation.5 | async-start | bytes 655360 | tf_op jit(solution)/shard_map/reduce_scatter | solution.py:295
Sparse Core Ops, SparseCore 0:
  168.2 37.1 all-gather.1
  268.4 126.4 all-reduce.1
  398.5 25.7 reduce-scatter.1

commit v2 on v1

--- a/solution.py
+++ b/solution.py
@@ -101,60 +101,188 @@
     )(page_info, own_info, queries, keys, values, keys_new, values_new)
 
 
-def place_kernel(placement, starts, fresh, incoming, out, buf, in_sems, out_sems):
-    slots, new_count, _ = fresh.shape
-    pages, page_len, _ = buf.shape
+def collect_kernel(order, keys, values, out, buf, in_sems, out_sems):
+    parts = in_sems.shape[0]
+    devices, _, per_peer = buf.shape[:3]
+    per_part = devices // parts
+    for part in range(parts):
+        for peer in range(part * per_part, (part + 1) * per_part):
+            for step in range(per_peer):
+                page = order[peer * per_peer + step]
+                for kind, pool in enumerate((keys, values)):
+                    pltpu.make_async_copy(
+                        pool.at[page], buf.at[peer, kind, step], in_sems.at[part]
+                    ).start()
+    for part in range(parts):
+        mine = pl.ds(part * per_part, per_part)
+        pltpu.make_async_copy(out.at[mine], buf.at[mine], in_sems.at[part]).wait()
+        pltpu.make_async_copy(buf.at[mine], out.at[mine], out_sems.at[part]).start()
+    for part in range(parts):
+        mine = pl.ds(part * per_part, per_part)
+        pltpu.make_async_copy(buf.at[mine], out.at[mine], out_sems.at[part]).wait()
+
+
+def collect(order, keys, values, devices):
+    pages, page_len, width = keys.shape
+    shape = (devices, 2, pages // devices, page_len, width)
+    parts = 16
+    whole = pl.BlockSpec(memory_space=pl.ANY)
+    return pl.pallas_call(
+        collect_kernel,
+        in_specs=[pl.BlockSpec(memory_space=pltpu.SMEM), whole, whole],
+        out_specs=whole,
+        out_shape=jax.ShapeDtypeStruct(shape, keys.dtype),
+        scratch_shapes=[
+            pltpu.VMEM(shape, keys.dtype),
+            pltpu.SemaphoreType.DMA((parts,)),
+            pltpu.SemaphoreType.DMA((parts,)),
+        ],
+        compiler_params=pltpu.CompilerParams(vmem_limit_bytes=VMEM_BYTES),
+        cost_estimate=pl.CostEstimate(
+            flops=0, bytes_accessed=8 * keys.size, transcendentals=0
+        ),
+        name="collect_pages",
+    )(order, keys, values)
+
+
+def place_kernel(
+    placement, starts, fresh_keys, fresh_values, incoming, out_keys, out_values, buf, in_sems, out_sems
+):
+    slots, new_count, _ = fresh_keys.shape
+    _, pages, page_len, _ = buf.shape
     per_slot = pages // slots
     for slot in range(slots):
         for step in range(per_slot):
             page = slot * per_slot + step
-            pltpu.make_async_copy(
-                incoming.at[placement[page]], buf.at[page], in_sems.at[slot]
-            ).start()
+            for kind in range(2):
+                pltpu.make_async_copy(
+                    incoming.at[placement[kind * pages + page]],
+                    buf.at[kind, page],
+                    in_sems.at[kind, slot],
+                ).start()
     for slot in range(slots):
         mine = pl.ds(slot * per_slot, per_slot)
-        pltpu.make_async_copy(incoming.at[mine], buf.at[mine], in_sems.at[slot]).wait()
-        for token in range(new_count):
-            spot = starts[slot] + token
-
-            @pl.when((spot >= 0) & (spot < per_slot * page_len))
-            def _():
-                page = slot * per_slot + spot // page_len
-                block = buf[page].astype(jnp.float32)
-                here = lax.broadcasted_iota(jnp.int32, block.shape, 0) == spot % page_len
-                row = fresh[slot, pl.ds(token, 1), :]
-                buf[page] = jnp.where(here, row, block).astype(buf.dtype)
-
-        pltpu.make_async_copy(buf.at[mine], out.at[mine], out_sems.at[slot]).start()
+        for kind, (fresh, out) in enumerate(((fresh_keys, out_keys), (fresh_values, out_values))):
+            pltpu.make_async_copy(out.at[mine], buf.at[kind, mine], in_sems.at[kind, slot]).wait()
+            for token in range(new_count):
+                spot = starts[slot] + token
+
+                @pl.when((spot >= 0) & (spot < per_slot * page_len))
+                def _():
+                    page = slot * per_slot + spot // page_len
+                    block = buf[kind, page].astype(jnp.float32)
+                    here = lax.broadcasted_iota(jnp.int32, block.shape, 0) == spot % page_len
+                    row = fresh[slot, pl.ds(token, 1), :]
+                    buf[kind, page] = jnp.where(here, row, block).astype(buf.dtype)
+
+            pltpu.make_async_copy(buf.at[kind, mine], out.at[mine], out_sems.at[kind, slot]).start()
     for slot in range(slots):
         mine = pl.ds(slot * per_slot, per_slot)
-        pltpu.make_async_copy(buf.at[mine], out.at[mine], out_sems.at[slot]).wait()
-
-
-def place(placement, starts, fresh, incoming, name):
-    slots = fresh.shape[0]
+        for kind, out in enumerate((out_keys, out_values)):
+            pltpu.make_async_copy(buf.at[kind, mine], out.at[mine], out_sems.at[kind, slot]).wait()
+
+
+def place(placement, starts, fresh_keys, fresh_values, incoming):
+    slots = fresh_keys.shape[0]
+    pages = incoming.shape[0] // 2
+    shape = (pages,) + incoming.shape[1:]
     smem = pl.BlockSpec(memory_space=pltpu.SMEM)
+    vmem = pl.BlockSpec(memory_space=pltpu.VMEM)
+    whole = pl.BlockSpec(memory_space=pl.ANY)
     return pl.pallas_call(
         place_kernel,
-        in_specs=[
-            smem,
-            smem,
-            pl.BlockSpec(memory_space=pltpu.VMEM),
-            pl.BlockSpec(memory_space=pl.ANY),
-        ],
-        out_specs=pl.BlockSpec(memory_space=pl.ANY),
-        out_shape=jax.ShapeDtypeStruct(incoming.shape, incoming.dtype),
+        in_specs=[smem, smem, vmem, vmem, whole],
+        out_specs=[whole, whole],
+        out_shape=[jax.ShapeDtypeStruct(shape, incoming.dtype)] * 2,
         scratch_shapes=[
-            pltpu.VMEM(incoming.shape, incoming.dtype),
-            pltpu.SemaphoreType.DMA((slots,)),
-            pltpu.SemaphoreType.DMA((slots,)),
+            pltpu.VMEM((2,) + shape, incoming.dtype),
+            pltpu.SemaphoreType.DMA((2, slots)),
+            pltpu.SemaphoreType.DMA((2, slots)),
         ],
         compiler_params=pltpu.CompilerParams(vmem_limit_bytes=VMEM_BYTES),
         cost_estimate=pl.CostEstimate(
-            flops=0, bytes_accessed=2 * incoming.size * 2, transcendentals=0
+            flops=0, bytes_accessed=4 * incoming.size, transcendentals=0
+        ),
+        name="place_pages",
+    )(placement, starts, fresh_keys, fresh_values, incoming)
+
+
+def push_kernel(sizes, spread, count, *refs):
+    srcs, outs = refs[:count], refs[count : 2 * count]
+    send_sems, recv_sems = refs[2 * count :]
+    total = math.prod(sizes.values())
+    me = 0
+    for name, size in sizes.items():
+        me = me * size + lax.axis_index(name)
+
+    def coords(flat):
+        found = {}
+        for name, size in reversed(sizes.items()):
+            found[name] = lax.rem(flat, size)
+            flat = lax.div(flat, size)
+        return found
+
+    barrier = pltpu.get_barrier_semaphore()
+
+    def greet(step, _):
+        peer = lax.rem(me + step, total)
+        pl.semaphore_signal(
+            barrier, inc=1, device_id=coords(peer), device_id_type=pl.DeviceIdType.MESH
+        )
+        return 0
+
+    lax.fori_loop(1, total, greet, 0)
+    pl.semaphore_wait(barrier, total - 1)
+
+    def copy(which, step, place):
+        peer = lax.rem(me + step, total)
+        src = srcs[which].at[peer] if spread else srcs[which]
+        return pltpu.make_async_remote_copy(
+            src_ref=src,
+            dst_ref=outs[which].at[place],
+            send_sem=send_sems.at[which, step],
+            recv_sem=recv_sems.at[which, step],
+            device_id=coords(peer),
+            device_id_type=pl.DeviceIdType.MESH,
+        )
+
+    def send(step, _):
+        for which in range(count):
+            copy(which, step, me).start()
+        return 0
+
+    lax.fori_loop(1, total, send, 0)
+    for which in range(count):
+        outs[which][me] = srcs[which][me] if spread else srcs[which][...]
+
+    def finish(step, _):
+        for which in range(count):
+            copy(which, step, lax.rem(me + total - step, total)).wait_recv()
+            copy(which, step, me).wait_send()
+        return 0
+
+    lax.fori_loop(1, total, finish, 0)
+
+
+def push(arrays, axes, spread, collective_id, name):
+    sizes = {axis: lax.axis_size(axis) for axis in axes}
+    total = math.prod(sizes.values())
+    vmem = pl.BlockSpec(memory_space=pltpu.VMEM)
+    shapes = [a.shape if spread else (total,) + a.shape for a in arrays]
+    return pl.pallas_call(
+        functools.partial(push_kernel, sizes, spread, len(arrays)),
+        in_specs=[vmem] * len(arrays),
+        out_specs=[vmem] * len(arrays),
+        out_shape=[jax.ShapeDtypeStruct(s, a.dtype) for s, a in zip(shapes, arrays)],
+        scratch_shapes=[
+            pltpu.SemaphoreType.DMA((len(arrays), total)),
+            pltpu.SemaphoreType.DMA((len(arrays), total)),
+        ],
+        compiler_params=pltpu.CompilerParams(
+            collective_id=collective_id, has_side_effects=True, vmem_limit_bytes=VMEM_BYTES // 2
         ),
         name=name,
-    )(placement, starts, fresh, incoming)
+    )(*arrays)
 
 
 def shards(
@@ -201,15 +329,7 @@
         jnp.where(send_rank[None, :] == local_pages[:, None], local_pages[None, :], 0), axis=1
     )
 
-    def move(pool):
-        outgoing = pool.at[send_order].get(mode="promise_in_bounds")
-        outgoing = outgoing.reshape(devices, per_peer, page_len, kv_width)
-        incoming = lax.all_to_all(outgoing, ("req", "seq"), split_axis=0, concat_axis=0, tiled=True)
-        return incoming.reshape(pages_dev, page_len, kv_width)
-
-    in_keys = move(pool_keys)
-    in_values = move(pool_values)
-
+    outgoing = collect(send_order, pool_keys, pool_values, devices)
     slots = jnp.arange(slot_total, dtype=i32)
     slot_owned = owner[None, :] == slots[:, None]
     slot_request = jnp.sum(jnp.where(slot_owned, slots[None, :], 0), axis=1)
@@ -220,14 +340,17 @@
     is_mine = my_requests[:, None, None] == slots[None, :, None]
     source = jnp.sum(jnp.where(is_mine, seq_pages[None], 0), axis=1).reshape(-1) // pages_dev
     ahead = (source[None, :] == source[:, None]) & (local_pages[None, :] < local_pages[:, None])
-    placement = source * per_peer + jnp.sum(ahead.astype(i32), axis=1)
+    placement = source * (2 * per_peer) + jnp.sum(ahead.astype(i32), axis=1)
+    placement = jnp.concatenate([placement, placement + per_peer])
 
     tokens_wide = new_tokens.astype(jnp.float32)
     square_mean = jnp.mean(tokens_wide * tokens_wide, axis=-1, keepdims=True)
     normed = (tokens_wide * lax.rsqrt(square_mean + NORM_EPS) * norm_gain).astype(jnp.bfloat16)
-    flat_rows = lax.all_gather(
-        normed.reshape(local_reqs * new_count, model_width), "req", axis=0, tiled=True
-    )
+    normed = normed.reshape(local_reqs * new_count, model_width)
+    normed, outgoing = lax.optimization_barrier((normed, outgoing))
+    incoming = lax.all_to_all(outgoing, ("req", "seq"), split_axis=0, concat_axis=0, tiled=True)
+    incoming = incoming.reshape(2 * pages_dev, page_len, kv_width)
+    flat_rows = push([normed], ("req",), False, 0, "gather_tokens")[0].reshape(-1, model_width)
     new_index = jnp.arange(new_count, dtype=i32)
     places = slot_lengths[:, None] + new_index[None, :]
     heads = lambda w: jnp.dot(flat_rows, w, preferred_element_type=jnp.float32)
@@ -236,7 +359,7 @@
     queries_now = rotate(queries_now, places).reshape(slot_total * new_count, query_cols)
     keys_now = rotate(keys_now, places).reshape(slot_total * new_count, key_cols)
     projected = jnp.concatenate([queries_now, keys_now, heads(w_value)], axis=-1)
-    every = lax.all_gather(projected.astype(jnp.bfloat16), "req", axis=0, tiled=False)
+    every = push([projected.astype(jnp.bfloat16)], ("req",), False, 1, "gather_heads")[0]
     own_kv = key_cols // HD
     queries = every[..., :query_cols].reshape(
         req_count, slot_total, new_count, own_kv, GROUPS, HD
@@ -277,28 +400,37 @@
     )
     peak = peak[..., 0]
     mass = mass[..., 0]
-    rows = peak.shape[1]
-    rescale = jnp.exp(peak - lax.pmax(peak, ("req", "seq")))
-    packed = jnp.concatenate(
-        [total * rescale[..., None], (mass * rescale).reshape(KVH, rows // HD, HD)], axis=1
-    ).astype(jnp.bfloat16)
-    packed = lax.psum(packed, ("req", "seq"))
-    packed = lax.dynamic_slice_in_dim(packed, req_index * own_kv, own_kv).astype(jnp.float32)
-    attended = packed[:, :rows] / packed[:, rows:].reshape(own_kv, rows, 1)
-    attended = attended.reshape(own_kv, slot_total, GROUPS, new_count, HD)
-    attended = (
-        jnp.transpose(attended, (1, 3, 0, 2, 4))
-        .reshape(slot_total * new_count, query_cols)
-        .astype(jnp.bfloat16)
-    )
+    seq_slots = slot_total // seq_count
+    part_rows = seq_slots * GROUPS * new_count
+
+    def by_device(part):
+        part = part.reshape((req_count, own_kv, seq_count, part_rows) + part.shape[2:])
+        part = jnp.swapaxes(part, 1, 2)
+        return part.reshape((devices, own_kv * part_rows) + part.shape[4:])
+
+    stats = jnp.stack([by_device(peak), by_device(mass)], axis=1)
+    stats = jnp.pad(stats, ((0, 0), (0, 6), (0, HD - own_kv * part_rows)))
+    parts, stats = push(
+        [by_device(total).astype(jnp.bfloat16), stats], ("req", "seq"), True, 2, "share_partials"
+    )
+    peaks = stats[:, 0, : own_kv * part_rows]
+    rescale = jnp.exp(peaks - jnp.max(peaks, axis=0))
+    mass = jnp.sum(stats[:, 1, : own_kv * part_rows] * rescale, axis=0)
+    attended = jnp.sum(parts.astype(jnp.float32) * rescale[..., None], axis=0) / mass[:, None]
+    attended = push([attended.astype(jnp.bfloat16)], ("seq",), False, 3, "gather_slots")[0]
+    attended = attended.reshape(seq_count, own_kv, seq_slots, GROUPS, new_count, HD)
+    attended = jnp.transpose(attended, (0, 2, 4, 1, 3, 5)).reshape(-1, query_cols)
     shares = jnp.dot(attended, w_out, preferred_element_type=jnp.float32).astype(jnp.bfloat16)
-    summed = lax.psum_scatter(shares, "req", scatter_dimension=0, tiled=True).astype(jnp.float32)
+    shares = shares.reshape(req_count, local_reqs * new_count, model_width)
+    shares = push([shares], ("req",), True, 4, "share_outputs")[0]
+    summed = jnp.sum(shares.astype(jnp.float32), axis=0)
     out_hidden = (tokens_wide + summed.reshape(tokens_wide.shape)).astype(jnp.bfloat16)
 
     starts = my_lengths - seq_index * positions
     out_shape = (local_reqs, positions, kv_width)
-    keys_out = place(placement, starts, of_mine(new_keys), in_keys, "place_keys")
-    values_out = place(placement, starts, of_mine(new_values), in_values, "place_values")
+    keys_out, values_out = place(
+        placement, starts, of_mine(new_keys), of_mine(new_values), incoming
+    )
     return (out_hidden, keys_out.reshape(out_shape), values_out.reshape(out_shape))
 
 

time: 442 us -> 257 us (0.58)
  waiting for transfers between devices: 278 us -> 0.01 us
  Pallas kernels: 21.8 us -> 207 us
  blocking collectives: 77.8 us -> 0 us
  between operations: 14.3 us -> 1.31 us
  local copies, waits for them, and re-layouts: 17.3 us -> 21.8 us
    pallas_call x2 -> x7, Pallas kernels: 8.79 us -> 194 us  [the longest x5 177 us: push(): pl.pallas_call(functools.partial(push_kernel, sizes, spread, len(arrays))...]
    psum x1 -> x0, waiting for transfers between devices: 126 us -> none  [shards(): packed = lax.psum(packed, ('req', 'seq'))]
    all_to_all x2 -> x1, waiting for transfers between devices: 89.8 us -> 0.01 us  [shards(): lax.all_to_all(outgoing, ('req', 'seq'), split_axis=0, concat_axis=0, til...]
    pmax x1 -> x0, blocking collectives: 40.8 us -> none  [shards(): rescale = jnp.exp(peak - lax.pmax(peak, ('req', 'seq')))]
    all_gather x1 -> x0, blocking collectives: 37 us -> none  [shards(): lax.all_gather(normed.reshape(local_reqs * new_count, model_width), 'req'...]
    all_gather x1 -> x0, waiting for transfers between devices: 36.6 us -> none  [shards(): lax.all_gather(projected.astype(jnp.bfloat16), 'req', axis=0, tiled=False)]
    reduce_scatter x1 -> x0, waiting for transfers between devices: 25.8 us -> none  [shards(): lax.psum_scatter(shares, 'req', scatter_dimension=0, tiled=True)]
    gather x2 -> x0, local copies, waits for them, and re-layouts: 10.1 us -> none  [move(): outgoing = pool.at[send_order].get(mode='promise_in_bounds')]
  transfers between devices with their start and end apart: 5 -> 1, of which waited for: 4 -> 0; matrix products, arithmetic and copies ran while one was open for 6% -> 10% of each run, Pallas kernels for 4% -> 74%
where the time goes in v2:
time: 257 us; the launch traced here: 256 us
  Pallas kernels  207 us (81%)
  local copies, waits for them, and re-layouts  21.8 us (8%)
  other arithmetic  13.5 us (5%)
  starting transfers between devices  7.61 us (3%)
  matrix products  5.09 us (2%)
    pallas_call x5, Pallas kernels, push(): pl.pallas_call(functools.partial(push_kernel, sizes, spread, len(arrays))...  177 us
    pallas_call x1, Pallas kernels, attend(): pl.pallas_call(functools.partial(attend_kernel, new_count), grid=(KVH,),...  13 us
    pallas_call x1, Pallas kernels, collect(): pl.pallas_call(collect_kernel, in_specs=[pl.BlockSpec(memory_space=pltpu....  10 us
    all_to_all x1, starting transfers between devices, shards(): lax.all_to_all(outgoing, ('req', 'seq'), split_axis=0, concat_axis=0, til...  7.61 us
    pallas_call x1, Pallas kernels, place(): pl.pallas_call(place_kernel, in_specs=[smem, smem, vmem, vmem, whole], ou...  7.29 us
    dot_general x3, local copies, waits for them, and re-layouts, shards(): heads = lambda w: jnp.dot(flat_rows, w, preferred_element_type=jnp.float32)  6.38 us
  transfers between devices with their start and end apart: 1, of which 0 were waited for; matrix products, arithmetic and copies ran while one was open for 10% of the time, Pallas kernels for 74%

profile of v2, /device:TPU:0, one launch (start us, length us, event | category | flops | bytes accessed | tf_op | source)
XLA Modules:
  0.0 256.1 jit_solution(15477620539098390616)
XLA Ops:
  0.7 0.9 constant_dynamic-slice_fusion
  1.7 0.7 fusion.16
  2.3 0.8 select_reduce_fusion.3
  3.1 0.1 dynamic_slice.15
  3.2 0.1 iota_compare_fusion.6
  3.3 0.2 select_reduce_fusion.1
  3.5 0.1 reshape.538
  3.6 1.1 fusion.4
  4.7 1.0 fusion.6
  5.8 3.3 %select_reduce_fusion = s32[128]{0:T(128)S(1)} fusion(s32[32,128]{1,0:T(8,128)S(1)} %add_add_fusion, s32[32,128]{1,0:T(8,128)} %param.21, s32[128]{0:T(128)S(1)} %iota_add_fusion), kind=kLoop, calls=%fused_computation.1 | loop fusion | flops 1572736 | bytes 33792 | tf_op jit(solution)/shard_map/reduce_sum | solution.py:326
  9.1 0.2 convert_reduce_fusion.2
  9.3 0.1 select_reduce_fusion.2.order
  9.4 2.2 copy-done.1
  11.6 10.0 %collect_pages.1 = bf16[32,2,4,16,1024]{4,3,2,1,0:T(8,128)(2,1)} custom-call(s32[128]{0:T(128)S(1)} %select_reduce_fusion.2.order, bf16[128,16,1024]{2,1,0:T(8,128)(2,1)S(1)} %copy-done.1, bf16[128,16,1024]{2,1,0:T(8,128)(2,1)} %values.1), custom_call_target="tpu_custom_call" | custom-call | bytes 16777216 | tf_op jit(solution)/shard_map/collect_pages/pallas_call | solution.py:130
  21.7 7.6 %all-to-all-start = ((bf16[32,2,4,16,1024]{4,3,2,1,0:T(8,128)(2,1)}), bf16[32,2,4,16,1024]{4,3,2,1,0:T(8,128)(2,1)}, u32[]{:S(2)}, u32[]{:S(2)}) async-start(bf16[32,2,4,16,1024]{4,3,2,1,0:T(8,128)(2,1)} %collect_pages.1), calls=%async_computation | async-start | bytes 16777216 | tf_op jit(solution)/shard_map/all_to_all | solution.py:351
  29.3 0.1 select_reduce_fusion.4
  29.4 0.1 fusion.8
  29.6 0.1 select_n.176.page_info
  29.7 0.1 select_n.179.own_info
  29.8 72.1 %gather_tokens.1 = bf16[4,32,2048]{2,1,0:T(8,128)(2,1)S(1)} custom-call(bf16[32,2048]{1,0:T(8,128)(2,1)S(1)} %reshape.524.refs_0_), custom_call_target="tpu_custom_call" | custom-call | tf_op jit(solution)/shard_map/gather_tokens/pallas_call | solution.py:272
  101.9 2.3 copy.63
  104.1 0.2 dot_general.22
  104.4 0.3 multiply_cosine_fusion
  104.7 1.8 fusion
  106.5 0.1 subtract_convert_fusion.1
  106.6 0.1 pad_maximum_fusion.4
  106.8 3.9 %copy.60 = bf16[512,2048]{1,0:T(8,128)(2,1)} copy(bf16[512,2048]{0,1:T(8,128)(2,1)} %bitcast.71) | data formatting | bytes 4194304 | tf_op jit(solution)/shard_map/dot_general | solution.py:356
  110.7 2.5 fusion.2
  113.2 0.1 subtract_convert_fusion
  113.4 0.1 pad_maximum_fusion.3
  113.6 0.3 convolution_convert_fusion.1
  114.0 22.7 %gather_heads.1 = bf16[4,128,1024]{2,1,0:T(8,128)(2,1)S(1)} custom-call(bf16[128,1024]{1,0:T(8,128)(2,1)S(1)} %pad_maximum_fusion.refs_0_), custom_call_target="tpu_custom_call" | custom-call | tf_op jit(solution)/shard_map/gather_heads/pallas_call | solution.py:272
  136.6 0.8 slice.47
  137.5 2.0 reshape.528
  139.4 1.3 copy.47
  140.7 0.1 fusion.19
  140.9 13.0 %attend_held_pages.1 = (f32[8,256,128]{2,1,0:T(8,128)S(1)}, f32[8,256,1]{2,1,0:T(8,128)S(1)}, f32[8,256,1]{2,1,0:T(8,128)S(1)}) custom-call(s32[1,2048]{1,0:T(1,128)S(1)} %select_n.176.page_info, s32[1,128]{1,0:T(1,128)S(1)} %select_n.179.own_info, bf16[8,256,128]{2,1,0:T(8,128)(2,1)S(1)} %bitcast.62, bf16[2048,1024]{1,0:T(8,128)(2,1)} %bitcast.60, ...), custom_call_target="tpu_custom_call" | custom-call | flops 2147483648 | bytes 8388608 | tf_op jit(solution)/shard_map/attend_held_pages/pallas_call | solution.py:76
  154.0 1.0 copy-done.4
  154.9 0.1 convert_element_type.65
  155.0 0.9 copy-done.3
  155.9 0.9 copy.48
  156.8 1.6 reduce.2
  158.4 0.1 stack_reshape.7
  158.5 1.6 reduce.1
  160.2 0.1 stack_reshape.6
  160.4 1.0 copy-done.2
  161.4 65.5 %share_partials.1 = (bf16[32,64,128]{2,1,0:T(8,128)(2,1)S(1)}, f32[32,8,128]{2,1,0:T(8,128)S(1)}) custom-call(bf16[32,64,128]{2,1,0:T(8,128)(2,1)S(1)} %bitcast.63, f32[32,8,128]{2,1,0:T(8,128)S(1)} %select_maximum_fusion.refs_1_), custom_call_target="tpu_custom_call" | custom-call | tf_op jit(solution)/shard_map/share_partials/pallas_call | solution.py:272
  227.0 0.3 multiply_reduce_fusion
  227.4 0.1 divide_convert_fusion.refs_0_
  227.5 6.9 %gather_slots.1 = bf16[8,64,128]{2,1,0:T(8,128)(2,1)S(1)} custom-call(bf16[64,128]{1,0:T(8,128)(2,1)S(1)} %divide_convert_fusion.refs_0_), custom_call_target="tpu_custom_call" | custom-call | tf_op jit(solution)/shard_map/gather_slots/pallas_call | solution.py:272
  234.3 0.1 copy.76
  234.5 0.4 convolution_convert_fusion
  235.0 9.4 %share_outputs.1 = bf16[4,32,2048]{2,1,0:T(8,128)(2,1)S(1)} custom-call(bf16[4,32,2048]{2,1,0:T(8,128)(2,1)S(1)} %bitcast.64), custom_call_target="tpu_custom_call" | custom-call | tf_op jit(solution)/shard_map/share_outputs/pallas_call | solution.py:272
  244.4 0.1 convert_reduce_fusion
  244.5 0.8 reshape.537
  245.2 0.7 fusion.18
  246.0 0.2 copy.64
  246.2 0.1 reshape.544.fresh_keys
  246.3 1.2 copy.65
  247.5 0.1 reshape.545.fresh_values
  247.6 0.1 dynamic-slice_subtract_fusion.starts
  247.7 0.2 convert_reduce_fusion.1
  247.9 0.7 fusion.7
  248.6 7.3 %place_pages.1 = (bf16[128,16,1024]{2,1,0:T(8,128)(2,1)}, bf16[128,16,1024]{2,1,0:T(8,128)(2,1)}) custom-call(s32[256]{0:T(256)S(1)} %pad_add_fusion.placement, s32[8]{0:T(128)S(1)} %dynamic-slice_subtract_fusion.starts, f32[8,4,1024]{2,1,0:T(4,128)S(1)} %reshape.544.fresh_keys, f32[8,4,1024]{2,1,0:T(4,128)S(1)} %reshape.545.fresh_values, ...), custom_call_target="tpu_custom_call" | custom-call | bytes 16777216 | tf_op jit(solution)/shard_map/place_pages/pallas_call | solution.py:192
  (46 shorter events, 1.0 us)
Async XLA Ops:
  0.6 233.9 %copy-start = (bf16[512,2048]{1,0:T(8,128)(2,1)S(1)}, bf16[512,2048]{1,0:T(8,128)(2,1)}, u32[]{:S(2)}) copy-start(bf16[512,2048]{1,0:T(8,128)(2,1)} %param.16) | copy-start | bytes 6291460
  9.4 2.2 copy-start.1
  21.7 227.0 %all-to-all-start = ((bf16[32,2,4,16,1024]{4,3,2,1,0:T(8,128)(2,1)}), bf16[32,2,4,16,1024]{4,3,2,1,0:T(8,128)(2,1)}, u32[]{:S(2)}, u32[]{:S(2)}) async-start(bf16[32,2,4,16,1024]{4,3,2,1,0:T(8,128)(2,1)} %collect_pages.1), calls=%async_computation | async-start | bytes 16777216 | tf_op jit(solution)/shard_map/all_to_all | solution.py:351
  110.7 2.9 %copy-start.6 = (bf16[2048,256]{1,0:T(8,128)(2,1)S(1)}, bf16[2048,256]{1,0:T(8,128)(2,1)}, u32[]{:S(2)}) copy-start(bf16[2048,256]{1,0:T(8,128)(2,1)} %param.15) | copy-start | bytes 3145732
  153.9 1.0 copy-start.4
  154.9 1.0 copy-start.3
  160.4 1.0 copy-start.2
  244.4 3.5 %copy-start.5 = (bf16[8,4,2048]{2,1,0:T(4,128)(2,1)S(1)}, bf16[8,4,2048]{2,1,0:T(4,128)(2,1)}, u32[]{:S(2)}) copy-start(bf16[8,4,2048]{2,1,0:T(4,128)(2,1)} %param.11) | copy-start | bytes 393220
  245.2 2.7 %copy-start.7 = (f32[8,4,2048]{2,1,0:T(4,128)S(1)}, f32[8,4,2048]{2,1,0:T(4,128)}, u32[]{:S(2)}) copy-start(f32[8,4,2048]{2,1,0:T(4,128)} %reshape.537) | copy-start | bytes 786436

commit v3 on v2

--- a/solution.py
+++ b/solution.py
@@ -105,18 +105,19 @@
     parts = in_sems.shape[0]
     devices, _, per_peer = buf.shape[:3]
     per_part = devices // parts
-    for part in range(parts):
-        for peer in range(part * per_part, (part + 1) * per_part):
-            for step in range(per_peer):
-                page = order[peer * per_peer + step]
-                for kind, pool in enumerate((keys, values)):
-                    pltpu.make_async_copy(
-                        pool.at[page], buf.at[peer, kind, step], in_sems.at[part]
-                    ).start()
-    for part in range(parts):
-        mine = pl.ds(part * per_part, per_part)
-        pltpu.make_async_copy(out.at[mine], buf.at[mine], in_sems.at[part]).wait()
-        pltpu.make_async_copy(buf.at[mine], out.at[mine], out_sems.at[part]).start()
+    for part in range(parts + 2):
+        if part < parts:
+            for peer in range(part * per_part, (part + 1) * per_part):
+                for step in range(per_peer):
+                    page = order[peer * per_peer + step]
+                    for kind, pool in enumerate((keys, values)):
+                        pltpu.make_async_copy(
+                            pool.at[page], buf.at[peer, kind, step], in_sems.at[part]
+                        ).start()
+        if part >= 2:
+            mine = pl.ds((part - 2) * per_part, per_part)
+            pltpu.make_async_copy(out.at[mine], buf.at[mine], in_sems.at[part - 2]).wait()
+            pltpu.make_async_copy(buf.at[mine], out.at[mine], out_sems.at[part - 2]).start()
     for part in range(parts):
         mine = pl.ds(part * per_part, per_part)
         pltpu.make_async_copy(buf.at[mine], out.at[mine], out_sems.at[part]).wait()
@@ -151,7 +152,8 @@
     slots, new_count, _ = fresh_keys.shape
     _, pages, page_len, _ = buf.shape
     per_slot = pages // slots
-    for slot in range(slots):
+
+    def fetch(slot):
         for step in range(per_slot):
             page = slot * per_slot + step
             for kind in range(2):
@@ -160,7 +162,8 @@
                     buf.at[kind, page],
                     in_sems.at[kind, slot],
                 ).start()
-    for slot in range(slots):
+
+    def finish(slot):
         mine = pl.ds(slot * per_slot, per_slot)
         for kind, (fresh, out) in enumerate(((fresh_keys, out_keys), (fresh_values, out_values))):
             pltpu.make_async_copy(out.at[mine], buf.at[kind, mine], in_sems.at[kind, slot]).wait()
@@ -176,6 +179,12 @@
                     buf[kind, page] = jnp.where(here, row, block).astype(buf.dtype)
 
             pltpu.make_async_copy(buf.at[kind, mine], out.at[mine], out_sems.at[kind, slot]).start()
+
+    for slot in range(slots + 2):
+        if slot < slots:
+            fetch(slot)
+        if slot >= 2:
+            finish(slot - 2)
     for slot in range(slots):
         mine = pl.ds(slot * per_slot, per_slot)
         for kind, out in enumerate((out_keys, out_values)):
@@ -347,10 +356,10 @@
     square_mean = jnp.mean(tokens_wide * tokens_wide, axis=-1, keepdims=True)
     normed = (tokens_wide * lax.rsqrt(square_mean + NORM_EPS) * norm_gain).astype(jnp.bfloat16)
     normed = normed.reshape(local_reqs * new_count, model_width)
-    normed, outgoing = lax.optimization_barrier((normed, outgoing))
+    flat_rows = push([normed], ("req",), False, 0, "gather_tokens")[0].reshape(-1, model_width)
+    flat_rows, outgoing = lax.optimization_barrier((flat_rows, outgoing))
     incoming = lax.all_to_all(outgoing, ("req", "seq"), split_axis=0, concat_axis=0, tiled=True)
     incoming = incoming.reshape(2 * pages_dev, page_len, kv_width)
-    flat_rows = push([normed], ("req",), False, 0, "gather_tokens")[0].reshape(-1, model_width)
     new_index = jnp.arange(new_count, dtype=i32)
     places = slot_lengths[:, None] + new_index[None, :]
     heads = lambda w: jnp.dot(flat_rows, w, preferred_element_type=jnp.float32)

time: 257 us -> 266 us (1.035)
  Pallas kernels: 207 us -> 221 us
  local copies, waits for them, and re-layouts: 21.8 us -> 15.4 us
    pallas_call x5, Pallas kernels: 177 us -> 192 us  [push(): pl.pallas_call(functools.partial(push_kernel, sizes, spread, len(arrays))...]
    dot_general x3 -> x0, local copies, waits for them, and re-layouts: 6.38 us -> none  [shards(): heads = lambda w: jnp.dot(flat_rows, w, preferred_element_type=jnp.float32)]
  transfers between devices with their start and end apart: 1 -> 1, of which waited for: 0 -> 0; matrix products, arithmetic and copies ran while one was open for 10% -> 8% of each run, Pallas kernels for 74% -> 74%
where the time goes in v3:
time: 266 us; the launch traced here: 264 us
  Pallas kernels  221 us (83%)
  local copies, waits for them, and re-layouts  15.4 us (6%)
  other arithmetic  14.3 us (5%)
  starting transfers between devices  6.01 us (2%)
  matrix products  5.55 us (2%)
    pallas_call x5, Pallas kernels, push(): pl.pallas_call(functools.partial(push_kernel, sizes, spread, len(arrays))...  192 us
    pallas_call x1, Pallas kernels, attend(): pl.pallas_call(functools.partial(attend_kernel, new_count), grid=(KVH,),...  13 us
    pallas_call x1, Pallas kernels, collect(): pl.pallas_call(collect_kernel, in_specs=[pl.BlockSpec(memory_space=pltpu....  8.45 us
    pallas_call x1, Pallas kernels, place(): pl.pallas_call(place_kernel, in_specs=[smem, smem, vmem, vmem, whole], ou...  7.67 us
    all_to_all x1, starting transfers between devices, shards(): lax.all_to_all(outgoing, ('req', 'seq'), split_axis=0, concat_axis=0, til...  6.01 us
  transfers between devices with their start and end apart: 1, of which 0 were waited for; matrix products, arithmetic and copies ran while one was open for 8% of the time, Pallas kernels for 74%

profile of v3, /device:TPU:0, one launch (start us, length us, event | category | flops | bytes accessed | tf_op | source)
XLA Modules:
  0.0 263.9 jit_solution(555282607169671200)
XLA Ops:
  0.7 0.9 constant_dynamic-slice_fusion
  1.7 0.7 fusion.12
  2.3 0.8 select_reduce_fusion.3
  3.1 0.1 dynamic_slice.15
  3.2 0.1 iota_compare_fusion.6
  3.3 0.2 select_reduce_fusion.1
  3.5 0.1 reshape.538
  3.6 1.1 fusion
  4.7 1.0 fusion.2
  5.8 10.7 %gather_tokens.1 = bf16[4,32,2048]{2,1,0:T(8,128)(2,1)S(1)} custom-call(bf16[32,2048]{1,0:T(8,128)(2,1)S(1)} %reshape.522.refs_0_), custom_call_target="tpu_custom_call" | custom-call | tf_op jit(solution)/shard_map/gather_tokens/pallas_call | solution.py:281
  16.4 0.1 add_add_fusion
  16.5 3.3 %select_reduce_fusion = s32[128]{0:T(128)S(1)} fusion(s32[32,128]{1,0:T(8,128)S(1)} %add_add_fusion, s32[32,128]{1,0:T(8,128)} %param.21, s32[128]{0:T(128)S(1)} %iota_add_fusion), kind=kLoop, calls=%fused_computation.1 | loop fusion | flops 1572736 | bytes 33792 | tf_op jit(solution)/shard_map/reduce_sum | solution.py:335
  19.8 0.2 convert_reduce_fusion.2
  20.0 0.1 select_reduce_fusion.2.order
  20.1 2.2 copy-done.1
  22.3 8.5 %collect_pages.1 = bf16[32,2,4,16,1024]{4,3,2,1,0:T(8,128)(2,1)} custom-call(s32[128]{0:T(128)S(1)} %select_reduce_fusion.2.order, bf16[128,16,1024]{2,1,0:T(8,128)(2,1)S(1)} %copy-done.1, bf16[128,16,1024]{2,1,0:T(8,128)(2,1)} %values.1), custom_call_target="tpu_custom_call" | custom-call | bytes 16777216 | tf_op jit(solution)/shard_map/collect_pages/pallas_call | solution.py:131
  30.8 6.0 %all-to-all-start = ((bf16[32,2,4,16,1024]{4,3,2,1,0:T(8,128)(2,1)}), bf16[32,2,4,16,1024]{4,3,2,1,0:T(8,128)(2,1)}, u32[]{:S(2)}, u32[]{:S(2)}) async-start(bf16[32,2,4,16,1024]{4,3,2,1,0:T(8,128)(2,1)} %collect_pages.1), calls=%async_computation | async-start | bytes 16777216 | tf_op jit(solution)/shard_map/all_to_all | solution.py:361
  36.8 0.1 select_reduce_fusion.4
  36.9 0.1 fusion.4
  37.0 0.1 select_n.176.page_info
  37.1 0.1 select_n.179.own_info
  37.2 1.5 fusion.17
  38.9 0.1 add_convert_fusion.2
  39.0 0.5 multiply_cosine_fusion
  39.5 0.3 subtract_convert_fusion.1
  39.8 0.2 pad_maximum_fusion.4
  40.0 2.0 fusion.16
  42.1 0.1 reshape.524
  42.2 0.3 subtract_convert_fusion
  42.5 0.2 pad_maximum_fusion.3
  42.7 1.5 convolution_convert_fusion.1
  44.3 76.5 %gather_heads.1 = bf16[4,128,1024]{2,1,0:T(8,128)(2,1)S(1)} custom-call(bf16[128,1024]{1,0:T(8,128)(2,1)S(1)} %pad_maximum_fusion.refs_0_), custom_call_target="tpu_custom_call" | custom-call | tf_op jit(solution)/shard_map/gather_heads/pallas_call | solution.py:281
  120.8 0.8 slice.47
  121.6 2.0 reshape.528
  123.5 1.3 copy.29
  124.9 0.1 fusion.15
  125.0 13.0 %attend_held_pages.1 = (f32[8,256,128]{2,1,0:T(8,128)S(1)}, f32[8,256,1]{2,1,0:T(8,128)S(1)}, f32[8,256,1]{2,1,0:T(8,128)S(1)}) custom-call(s32[1,2048]{1,0:T(1,128)S(1)} %select_n.176.page_info, s32[1,128]{1,0:T(1,128)S(1)} %select_n.179.own_info, bf16[8,256,128]{2,1,0:T(8,128)(2,1)S(1)} %bitcast.56, bf16[2048,1024]{1,0:T(8,128)(2,1)} %bitcast.52, ...), custom_call_target="tpu_custom_call" | custom-call | flops 2147483648 | bytes 8388608 | tf_op jit(solution)/shard_map/attend_held_pages/pallas_call | solution.py:76
  138.1 1.0 copy-done.4
  139.0 0.1 convert_element_type.65
  139.1 0.9 copy-done.3
  140.0 0.9 copy.30
  140.9 1.6 reduce.2
  142.5 0.1 stack_reshape.7
  142.6 1.6 reduce.1
  144.3 0.1 stack_reshape.6
  144.5 1.0 copy-done.2
  145.5 89.7 %share_partials.1 = (bf16[32,64,128]{2,1,0:T(8,128)(2,1)S(1)}, f32[32,8,128]{2,1,0:T(8,128)S(1)}) custom-call(bf16[32,64,128]{2,1,0:T(8,128)(2,1)S(1)} %bitcast.57, f32[32,8,128]{2,1,0:T(8,128)S(1)} %select_maximum_fusion.refs_1_), custom_call_target="tpu_custom_call" | custom-call | tf_op jit(solution)/shard_map/share_partials/pallas_call | solution.py:281
  235.4 0.3 multiply_reduce_fusion
  235.7 0.1 divide_convert_fusion.refs_0_
  235.8 6.0 %gather_slots.1 = bf16[8,64,128]{2,1,0:T(8,128)(2,1)S(1)} custom-call(bf16[64,128]{1,0:T(8,128)(2,1)S(1)} %divide_convert_fusion.refs_0_), custom_call_target="tpu_custom_call" | custom-call | tf_op jit(solution)/shard_map/gather_slots/pallas_call | solution.py:281
  241.8 0.1 copy.46
  242.0 0.4 convolution_convert_fusion
  242.5 9.3 %share_outputs.1 = bf16[4,32,2048]{2,1,0:T(8,128)(2,1)S(1)} custom-call(bf16[4,32,2048]{2,1,0:T(8,128)(2,1)S(1)} %bitcast.58), custom_call_target="tpu_custom_call" | custom-call | tf_op jit(solution)/shard_map/share_outputs/pallas_call | solution.py:281
  251.9 0.1 convert_reduce_fusion
  251.9 0.8 reshape.537
  252.7 0.7 fusion.14
  253.5 0.2 copy.38
  253.7 0.1 reshape.544.fresh_keys
  253.8 1.2 copy.39
  255.0 0.1 reshape.545.fresh_values
  255.1 0.1 dynamic-slice_subtract_fusion.starts
  255.2 0.2 convert_reduce_fusion.1
  255.4 0.7 fusion.3
  256.1 7.7 %place_pages.1 = (bf16[128,16,1024]{2,1,0:T(8,128)(2,1)}, bf16[128,16,1024]{2,1,0:T(8,128)(2,1)}) custom-call(s32[256]{0:T(256)S(1)} %pad_add_fusion.placement, s32[8]{0:T(128)S(1)} %dynamic-slice_subtract_fusion.starts, f32[8,4,1024]{2,1,0:T(4,128)S(1)} %reshape.544.fresh_keys, f32[8,4,1024]{2,1,0:T(4,128)S(1)} %reshape.545.fresh_values, ...), custom_call_target="tpu_custom_call" | custom-call | bytes 16777216 | tf_op jit(solution)/shard_map/place_pages/pallas_call | solution.py:201
  (41 shorter events, 0.8 us)
Async XLA Ops:
  0.6 241.4 %copy-start = (bf16[512,2048]{1,0:T(8,128)(2,1)S(1)}, bf16[512,2048]{1,0:T(8,128)(2,1)}, u32[]{:S(2)}) copy-start(bf16[512,2048]{1,0:T(8,128)(2,1)} %param.16) | copy-start | bytes 6291460
  20.1 2.2 copy-start.1
  30.8 225.4 %all-to-all-start = ((bf16[32,2,4,16,1024]{4,3,2,1,0:T(8,128)(2,1)}), bf16[32,2,4,16,1024]{4,3,2,1,0:T(8,128)(2,1)}, u32[]{:S(2)}, u32[]{:S(2)}) async-start(bf16[32,2,4,16,1024]{4,3,2,1,0:T(8,128)(2,1)} %collect_pages.1), calls=%async_computation | async-start | bytes 16777216 | tf_op jit(solution)/shard_map/all_to_all | solution.py:361
  138.1 1.0 copy-start.4
  139.0 1.0 copy-start.3
  144.5 1.0 copy-start.2
  251.8 3.5 %copy-start.5 = (bf16[8,4,2048]{2,1,0:T(4,128)(2,1)S(1)}, bf16[8,4,2048]{2,1,0:T(4,128)(2,1)}, u32[]{:S(2)}) copy-start(bf16[8,4,2048]{2,1,0:T(4,128)(2,1)} %param.11) | copy-start | bytes 393220
  252.7 2.7 %copy-start.6 = (f32[8,4,2048]{2,1,0:T(4,128)S(1)}, f32[8,4,2048]{2,1,0:T(4,128)}, u32[]{:S(2)}) copy-start(f32[8,4,2048]{2,1,0:T(4,128)} %reshape.537) | copy-start | bytes 786436

commit v4 on v3

--- a/solution.py
+++ b/solution.py
@@ -216,18 +216,20 @@
     )(placement, starts, fresh_keys, fresh_values, incoming)
 
 
-def push_kernel(sizes, spread, count, *refs):
+def push_kernel(digits, spread, count, *refs):
     srcs, outs = refs[:count], refs[count : 2 * count]
     send_sems, recv_sems = refs[2 * count :]
-    total = math.prod(sizes.values())
+    total = math.prod(size for _, _, size in digits)
     me = 0
-    for name, size in sizes.items():
-        me = me * size + lax.axis_index(name)
+    for name, stride, size in digits:
+        me = me * size + lax.rem(lax.div(lax.axis_index(name), stride), size)
 
     def coords(flat):
         found = {}
-        for name, size in reversed(sizes.items()):
-            found[name] = lax.rem(flat, size)
+        for name, stride, size in reversed(digits):
+            index = found.get(name, lax.axis_index(name))
+            mine = lax.rem(lax.div(lax.axis_index(name), stride), size)
+            found[name] = index + (lax.rem(flat, size) - mine) * stride
             flat = lax.div(flat, size)
         return found
 
@@ -273,13 +275,12 @@
     lax.fori_loop(1, total, finish, 0)
 
 
-def push(arrays, axes, spread, collective_id, name):
-    sizes = {axis: lax.axis_size(axis) for axis in axes}
-    total = math.prod(sizes.values())
+def push(arrays, digits, spread, collective_id, name):
+    total = math.prod(size for _, _, size in digits)
     vmem = pl.BlockSpec(memory_space=pltpu.VMEM)
     shapes = [a.shape if spread else (total,) + a.shape for a in arrays]
     return pl.pallas_call(
-        functools.partial(push_kernel, sizes, spread, len(arrays)),
+        functools.partial(push_kernel, tuple(digits), spread, len(arrays)),
         in_specs=[vmem] * len(arrays),
         out_specs=[vmem] * len(arrays),
         out_shape=[jax.ShapeDtypeStruct(s, a.dtype) for s, a in zip(shapes, arrays)],
@@ -322,6 +323,9 @@
     per_peer = pages_dev // devices
     query_cols = w_query.shape[1]
     key_cols = w_key.shape[1]
+    low_count = 2 if seq_count % 2 == 0 else 1
+    high_count = seq_count // low_count
+    over_req = [("req", 1, req_count)]
     i32 = jnp.int32
     local_pages = jnp.arange(pages_dev, dtype=i32)
 
@@ -356,10 +360,10 @@
     square_mean = jnp.mean(tokens_wide * tokens_wide, axis=-1, keepdims=True)
     normed = (tokens_wide * lax.rsqrt(square_mean + NORM_EPS) * norm_gain).astype(jnp.bfloat16)
     normed = normed.reshape(local_reqs * new_count, model_width)
-    flat_rows = push([normed], ("req",), False, 0, "gather_tokens")[0].reshape(-1, model_width)
-    flat_rows, outgoing = lax.optimization_barrier((flat_rows, outgoing))
+    normed, outgoing = lax.optimization_barrier((normed, outgoing))
     incoming = lax.all_to_all(outgoing, ("req", "seq"), split_axis=0, concat_axis=0, tiled=True)
     incoming = incoming.reshape(2 * pages_dev, page_len, kv_width)
+    flat_rows = push([normed], over_req, False, 0, "gather_tokens")[0].reshape(-1, model_width)
     new_index = jnp.arange(new_count, dtype=i32)
     places = slot_lengths[:, None] + new_index[None, :]
     heads = lambda w: jnp.dot(flat_rows, w, preferred_element_type=jnp.float32)
@@ -368,7 +372,7 @@
     queries_now = rotate(queries_now, places).reshape(slot_total * new_count, query_cols)
     keys_now = rotate(keys_now, places).reshape(slot_total * new_count, key_cols)
     projected = jnp.concatenate([queries_now, keys_now, heads(w_value)], axis=-1)
-    every = push([projected.astype(jnp.bfloat16)], ("req",), False, 1, "gather_heads")[0]
+    every = push([projected.astype(jnp.bfloat16)], over_req, False, 1, "gather_heads")[0]
     own_kv = key_cols // HD
     queries = every[..., :query_cols].reshape(
         req_count, slot_total, new_count, own_kv, GROUPS, HD
@@ -412,26 +416,39 @@
     seq_slots = slot_total // seq_count
     part_rows = seq_slots * GROUPS * new_count
 
-    def by_device(part):
-        part = part.reshape((req_count, own_kv, seq_count, part_rows) + part.shape[2:])
-        part = jnp.swapaxes(part, 1, 2)
-        return part.reshape((devices, own_kv * part_rows) + part.shape[4:])
-
-    stats = jnp.stack([by_device(peak), by_device(mass)], axis=1)
-    stats = jnp.pad(stats, ((0, 0), (0, 6), (0, HD - own_kv * part_rows)))
-    parts, stats = push(
-        [by_device(total).astype(jnp.bfloat16), stats], ("req", "seq"), True, 2, "share_partials"
-    )
-    peaks = stats[:, 0, : own_kv * part_rows]
-    rescale = jnp.exp(peaks - jnp.max(peaks, axis=0))
-    mass = jnp.sum(stats[:, 1, : own_kv * part_rows] * rescale, axis=0)
-    attended = jnp.sum(parts.astype(jnp.float32) * rescale[..., None], axis=0) / mass[:, None]
-    attended = push([attended.astype(jnp.bfloat16)], ("seq",), False, 3, "gather_slots")[0]
+    def by_plane(part):
+        part = part.reshape((req_count, own_kv, high_count, low_count, part_rows) + part.shape[2:])
+        part = jnp.transpose(part, (0, 3, 2, 1, 4) + tuple(range(5, part.ndim)))
+        return part.reshape((req_count * low_count, high_count * own_kv * part_rows) + part.shape[5:])
+
+    def exchange(parts, peaks, masses, digits, collective_id, name):
+        count = peaks.shape[1]
+        stats = jnp.stack([peaks, masses], axis=1)
+        stats = jnp.pad(stats, ((0, 0), (0, 6), (0, -count % HD)))
+        parts, stats = push([parts.astype(jnp.bfloat16), stats], digits, True, collective_id, name)
+        peaks = stats[:, 0, :count]
+        top = jnp.max(peaks, axis=0)
+        rescale = jnp.exp(peaks - top)
+        masses = jnp.sum(stats[:, 1, :count] * rescale, axis=0)
+        return jnp.sum(parts.astype(jnp.float32) * rescale[..., None], axis=0), top, masses
+
+    plane = [("req", 1, req_count), ("seq", 1, low_count)]
+    column = [("seq", low_count, high_count)]
+    total, peak, mass = exchange(
+        by_plane(total), by_plane(peak), by_plane(mass), plane, 2, "share_in_plane"
+    )
+    split = lambda part: part.reshape((high_count, own_kv * part_rows) + part.shape[1:])
+    total, peak, mass = exchange(
+        split(total), split(peak), split(mass), column, 5, "share_in_column"
+    )
+    attended = total / mass[:, None]
+    over_seq = [("seq", 1, seq_count)]
+    attended = push([attended.astype(jnp.bfloat16)], over_seq, False, 3, "gather_slots")[0]
     attended = attended.reshape(seq_count, own_kv, seq_slots, GROUPS, new_count, HD)
     attended = jnp.transpose(attended, (0, 2, 4, 1, 3, 5)).reshape(-1, query_cols)
     shares = jnp.dot(attended, w_out, preferred_element_type=jnp.float32).astype(jnp.bfloat16)
     shares = shares.reshape(req_count, local_reqs * new_count, model_width)
-    shares = push([shares], ("req",), True, 4, "share_outputs")[0]
+    shares = lax.all_to_all(shares, "req", split_axis=0, concat_axis=0, tiled=True)
     summed = jnp.sum(shares.astype(jnp.float32), axis=0)
     out_hidden = (tokens_wide + summed.reshape(tokens_wide.shape)).astype(jnp.bfloat16)
 

time: 266 us -> 326 us (1.23)
  waiting for transfers between devices: 0.01 us -> 183 us
  Pallas kernels: 221 us -> 77.4 us
  blocking collectives: 0 us -> 12.3 us
  local copies, waits for them, and re-layouts: 15.4 us -> 22.8 us
  other arithmetic: 14.3 us -> 17.8 us
    all_to_all x1, waiting for transfers between devices: 0.01 us -> 183 us  [shards(): lax.all_to_all(outgoing, ('req', 'seq'), split_axis=0, concat_axis=0, til...]
    pallas_call x5, Pallas kernels: 192 us -> 48 us  [push(): pl.pallas_call(functools.partial(push_kernel, tuple(digits), spread, len(...]
    all_to_all x0 -> x1, blocking collectives: none -> 12.3 us  [shards(): lax.all_to_all(shares, 'req', split_axis=0, concat_axis=0, tiled=True)]
    dot_general x0 -> x3, local copies, waits for them, and re-layouts: none -> 6.38 us  [shards(): heads = lambda w: jnp.dot(flat_rows, w, preferred_element_type=jnp.float32)]
  transfers between devices with their start and end apart: 1 -> 1, of which waited for: 0 -> 1; matrix products, arithmetic and copies ran while one was open for 8% -> 1% of each run, Pallas kernels for 74% -> 0%
where the time goes in v4:
time: 326 us; the launch traced here: 324 us
  waiting for transfers between devices  183 us (56%)
  Pallas kernels  77.4 us (24%)
  local copies, waits for them, and re-layouts  22.8 us (7%)
  other arithmetic  17.8 us (5%)
  blocking collectives  12.3 us (4%)
  matrix products  5.08 us (2%)
  starting transfers between devices  4.21 us (1%)
    all_to_all x1, waiting for transfers between devices, shards(): lax.all_to_all(outgoing, ('req', 'seq'), split_axis=0, concat_axis=0, til...  183 us
    pallas_call x5, Pallas kernels, push(): pl.pallas_call(functools.partial(push_kernel, tuple(digits), spread, len(...  48 us
    pallas_call x1, Pallas kernels, attend(): pl.pallas_call(functools.partial(attend_kernel, new_count), grid=(KVH,),...  13 us
    all_to_all x1, blocking collectives, shards(): lax.all_to_all(shares, 'req', split_axis=0, concat_axis=0, tiled=True)  12.3 us
    pallas_call x1, Pallas kernels, collect(): pl.pallas_call(collect_kernel, in_specs=[pl.BlockSpec(memory_space=pltpu....  8.65 us
    pallas_call x1, Pallas kernels, place(): pl.pallas_call(place_kernel, in_specs=[smem, smem, vmem, vmem, whole], ou...  7.67 us
  transfers between devices with their start and end apart: 1, of which 1 were waited for; matrix products, arithmetic and copies ran while one was open for 1% of the time, Pallas kernels for 0%

profile of v4, /device:TPU:0, one launch (start us, length us, event | category | flops | bytes accessed | tf_op | source)
XLA Modules:
  0.0 323.8 jit_solution(10582581251409972115)
XLA Ops:
  0.7 0.9 constant_dynamic-slice_fusion
  1.7 0.7 fusion.18
  2.3 0.8 select_reduce_fusion.3
  3.3 0.2 select_reduce_fusion.1
  3.6 0.5 and_select_fusion
  4.2 3.3 %select_reduce_fusion = s32[128]{0:T(128)S(1)} fusion(s32[32,128]{1,0:T(8,128)S(1)} %add_add_fusion, s32[32,128]{1,0:T(8,128)} %param.21, s32[128]{0:T(128)S(1)} %iota_add_fusion), kind=kLoop, calls=%fused_computation.1 | loop fusion | flops 1572736 | bytes 33792 | tf_op jit(solution)/shard_map/reduce_sum | solution.py:339
  7.5 0.5 fusion.17
  8.0 0.2 convert_reduce_fusion.2
  8.2 1.1 fusion.4
  9.3 1.0 fusion.6
  10.4 0.1 select_reduce_fusion.2.order
  10.5 2.2 copy-done.1
  12.7 8.6 %collect_pages.1 = bf16[32,2,4,16,1024]{4,3,2,1,0:T(8,128)(2,1)} custom-call(s32[128]{0:T(128)S(1)} %select_reduce_fusion.2.order, bf16[128,16,1024]{2,1,0:T(8,128)(2,1)S(1)} %copy-done.1, bf16[128,16,1024]{2,1,0:T(8,128)(2,1)} %values.1), custom_call_target="tpu_custom_call" | custom-call | bytes 16777216 | tf_op jit(solution)/shard_map/collect_pages/pallas_call | solution.py:131
  21.3 10.7 %gather_tokens.1 = bf16[4,32,2048]{2,1,0:T(8,128)(2,1)S(1)} custom-call(bf16[32,2048]{1,0:T(8,128)(2,1)S(1)} %reshape.543.refs_0_), custom_call_target="tpu_custom_call" | custom-call | tf_op jit(solution)/shard_map/gather_tokens/pallas_call | solution.py:282
  32.0 2.3 copy.66
  34.3 0.2 dot_general.22
  34.5 1.8 fusion
  36.3 0.3 multiply_cosine_fusion
  36.6 0.1 subtract_convert_fusion.1
  36.7 0.1 pad_maximum_fusion.4
  36.9 3.9 %copy.63 = bf16[512,2048]{1,0:T(8,128)(2,1)} copy(bf16[512,2048]{0,1:T(8,128)(2,1)} %bitcast.81) | data formatting | bytes 4194304 | tf_op jit(solution)/shard_map/dot_general | solution.py:369
  40.8 2.5 fusion.2
  43.3 0.1 subtract_convert_fusion
  43.5 0.1 pad_maximum_fusion.3
  43.7 0.3 convolution_convert_fusion.1
  44.1 14.9 %gather_heads.1 = bf16[4,128,1024]{2,1,0:T(8,128)(2,1)S(1)} custom-call(bf16[128,1024]{1,0:T(8,128)(2,1)S(1)} %pad_maximum_fusion.refs_0_), custom_call_target="tpu_custom_call" | custom-call | tf_op jit(solution)/shard_map/gather_heads/pallas_call | solution.py:282
  59.0 0.8 slice.53
  59.8 0.8 fusion.22
  60.7 0.7 fusion.8
  61.4 0.9 select_n.176.page_info
  62.3 0.6 iota_select_fusion
  63.0 0.8 select_n.179.own_info
  63.8 2.0 reshape.547
  65.7 1.3 copy.49
  67.1 0.9 pad_maximum_fusion.1
  68.0 13.0 %attend_held_pages.1 = (f32[8,256,128]{2,1,0:T(8,128)S(1)}, f32[8,256,1]{2,1,0:T(8,128)S(1)}, f32[8,256,1]{2,1,0:T(8,128)S(1)}) custom-call(s32[1,2048]{1,0:T(1,128)S(1)} %select_n.176.page_info, s32[1,128]{1,0:T(1,128)S(1)} %select_n.179.own_info, bf16[8,256,128]{2,1,0:T(8,128)(2,1)S(1)} %bitcast.72, bf16[2048,1024]{1,0:T(8,128)(2,1)} %bitcast.70, ...), custom_call_target="tpu_custom_call" | custom-call | flops 2147483648 | bytes 8388608 | tf_op jit(solution)/shard_map/attend_held_pages/pallas_call | solution.py:76
  81.1 1.0 copy-done.4
  82.1 0.9 copy-done.3
  83.0 0.9 copy.50
  83.9 1.6 reduce.3
  85.5 0.1 reshape_squeeze.7
  85.6 0.1 stack_reshape.13
  85.7 1.6 reduce.2
  87.3 0.1 reshape_squeeze.6
  87.4 0.1 stack_reshape.12
  87.5 1.0 copy-done.2
  88.6 8.6 %share_in_plane.1 = (bf16[8,256,128]{2,1,0:T(8,128)(2,1)S(1)}, f32[8,8,256]{2,1,0:T(8,128)S(1)}) custom-call(bf16[8,256,128]{2,1,0:T(8,128)(2,1)S(1)} %bitcast.73, f32[8,8,256]{2,1,0:T(8,128)S(1)} %select_maximum_fusion.refs_1_), custom_call_target="tpu_custom_call" | custom-call | tf_op jit(solution)/shard_map/share_in_plane/pallas_call | solution.py:282
  97.2 0.8 copy-done.5
  98.2 1.4 multiply_reduce_fusion
  99.6 7.0 %share_in_column.1 = (bf16[4,64,128]{2,1,0:T(8,128)(2,1)S(1)}, f32[4,8,128]{2,1,0:T(8,128)S(1)}) custom-call(bf16[4,64,128]{2,1,0:T(8,128)(2,1)S(1)} %bitcast.77, f32[4,8,128]{2,1,0:T(8,128)S(1)} %select_maximum_fusion.1.refs_1_), custom_call_target="tpu_custom_call" | custom-call | tf_op jit(solution)/shard_map/share_in_column/pallas_call | solution.py:282
  106.7 0.1 multiply_reduce_fusion.1
  106.9 6.9 %gather_slots.1 = bf16[8,64,128]{2,1,0:T(8,128)(2,1)S(1)} custom-call(bf16[64,128]{1,0:T(8,128)(2,1)S(1)} %divide_convert_fusion.refs_0_), custom_call_target="tpu_custom_call" | custom-call | tf_op jit(solution)/shard_map/gather_slots/pallas_call | solution.py:282
  113.9 0.1 copy.81
  114.0 0.4 convolution_convert_fusion
  114.5 12.3 %all_to_all.10 = bf16[4,32,2048]{2,1,0:T(8,128)(2,1)} all-to-all(bf16[4,32,2048]{2,1,0:T(8,128)(2,1)S(1)} %bitcast.85), channel_id=1, replica_groups=mesh['req'=4,'seq'=8] {'req'}, dimensions={0} | all-to-all | bytes 1048576 | tf_op jit(solution)/shard_map/all_to_all | solution.py:451
  126.8 4.2 %all-to-all-start.1 = ((bf16[32,2,4,16,1024]{4,3,2,1,0:T(8,128)(2,1)}), bf16[32,2,4,16,1024]{4,3,2,1,0:T(8,128)(2,1)}, u32[]{:S(2)}, u32[]{:S(2)}) async-start(bf16[32,2,4,16,1024]{4,3,2,1,0:T(8,128)(2,1)} %collect_pages.1), calls=%async_computation.1 | async-start | bytes 16777216 | tf_op jit(solution)/shard_map/all_to_all | solution.py:364
  131.1 0.2 copy.67
  131.3 0.1 reshape.563.fresh_keys
  131.4 0.2 copy.68
  131.9 0.2 convert_reduce_fusion.1
  132.1 0.1 copy-done.6
  132.3 0.7 fusion.7
  133.1 182.9 %all-to-all-done.1 = bf16[32,2,4,16,1024]{4,3,2,1,0:T(8,128)(2,1)} async-done(((bf16[32,2,4,16,1024]{4,3,2,1,0:T(8,128)(2,1)}), bf16[32,2,4,16,1024]{4,3,2,1,0:T(8,128)(2,1)}, u32[]{:S(2)}, u32[]{:S(2)}) %all-to-all-start.1) | async-done | bytes 8388640 | tf_op jit(solution)/shard_map/all_to_all | solution.py:364
  315.9 7.7 %place_pages.1 = (bf16[128,16,1024]{2,1,0:T(8,128)(2,1)}, bf16[128,16,1024]{2,1,0:T(8,128)(2,1)}) custom-call(s32[256]{0:T(256)S(1)} %pad_add_fusion.placement, s32[8]{0:T(128)S(1)} %dynamic-slice_subtract_fusion.starts, f32[8,4,1024]{2,1,0:T(4,128)S(1)} %reshape.563.fresh_keys, f32[8,4,1024]{2,1,0:T(4,128)S(1)} %reshape.564.fresh_values, ...), custom_call_target="tpu_custom_call" | custom-call | bytes 16777216 | tf_op jit(solution)/shard_map/place_pages/pallas_call | solution.py:201
  (67 shorter events, 1.8 us)
Async XLA Ops:
  0.6 113.4 %copy-start = (bf16[512,2048]{1,0:T(8,128)(2,1)S(1)}, bf16[512,2048]{1,0:T(8,128)(2,1)}, u32[]{:S(2)}) copy-start(bf16[512,2048]{1,0:T(8,128)(2,1)} %param.16) | copy-start | bytes 6291460
  7.5 1.8 copy-start.9
  10.5 2.2 copy-start.1
  40.8 2.9 copy-start.8
  44.0 16.5 %copy-start.10 = (s32[128]{0:T(128)S(1)}, s32[128]{0:T(128)}, u32[]{:S(2)}) copy-start(s32[128]{0:T(128)} %copy-done.9) | copy-start | bytes 1540
  44.0 16.5 %copy-start.13 = (s32[128]{0:T(128)S(1)}, s32[128]{0:T(128)}, u32[]{:S(2)}) copy-start(s32[128]{0:T(128)} %get-tuple-element.34) | copy-start | bytes 1540
  44.1 16.6 %copy-start.11 = (s32[128]{0:T(128)S(1)}, s32[128]{0:T(128)}, u32[]{:S(2)}) copy-start(s32[128]{0:T(128)} %get-tuple-element.33) | copy-start | bytes 1540
  81.1 1.0 copy-start.4
  82.0 1.0 copy-start.3
  87.5 1.0 copy-start.2
  97.2 0.8 copy-start.5
  126.8 189.1 %all-to-all-start.1 = ((bf16[32,2,4,16,1024]{4,3,2,1,0:T(8,128)(2,1)}), bf16[32,2,4,16,1024]{4,3,2,1,0:T(8,128)(2,1)}, u32[]{:S(2)}, u32[]{:S(2)}) async-start(bf16[32,2,4,16,1024]{4,3,2,1,0:T(8,128)(2,1)} %collect_pages.1), calls=%async_computation.1 | async-start | bytes 16777216 | tf_op jit(solution)/shard_map/all_to_all | solution.py:364
  131.0 0.8 copy-start.12
  131.0 1.3 copy-start.7
  131.1 1.1 copy-start.6

commit v5 on v4

--- a/solution.py
+++ b/solution.py
@@ -421,11 +421,12 @@
         part = jnp.transpose(part, (0, 3, 2, 1, 4) + tuple(range(5, part.ndim)))
         return part.reshape((req_count * low_count, high_count * own_kv * part_rows) + part.shape[5:])
 
-    def exchange(parts, peaks, masses, digits, collective_id, name):
-        count = peaks.shape[1]
-        stats = jnp.stack([peaks, masses], axis=1)
-        stats = jnp.pad(stats, ((0, 0), (0, 6), (0, -count % HD)))
-        parts, stats = push([parts.astype(jnp.bfloat16), stats], digits, True, collective_id, name)
+    def exchange(parts, peaks, masses, digits, spread, collective_id, name):
+        count = peaks.shape[-1]
+        stats = jnp.stack([peaks, masses], axis=-2)
+        wide = ((0, 0),) * (stats.ndim - 2)
+        stats = jnp.pad(stats, wide + ((0, 6), (0, -count % HD)))
+        parts, stats = push([parts.astype(jnp.bfloat16), stats], digits, spread, collective_id, name)
         peaks = stats[:, 0, :count]
         top = jnp.max(peaks, axis=0)
         rescale = jnp.exp(peaks - top)
@@ -435,21 +436,21 @@
     plane = [("req", 1, req_count), ("seq", 1, low_count)]
     column = [("seq", low_count, high_count)]
     total, peak, mass = exchange(
-        by_plane(total), by_plane(peak), by_plane(mass), plane, 2, "share_in_plane"
-    )
-    split = lambda part: part.reshape((high_count, own_kv * part_rows) + part.shape[1:])
-    total, peak, mass = exchange(
-        split(total), split(peak), split(mass), column, 5, "share_in_column"
-    )
-    attended = total / mass[:, None]
-    over_seq = [("seq", 1, seq_count)]
-    attended = push([attended.astype(jnp.bfloat16)], over_seq, False, 3, "gather_slots")[0]
-    attended = attended.reshape(seq_count, own_kv, seq_slots, GROUPS, new_count, HD)
+        by_plane(total), by_plane(peak), by_plane(mass), plane, True, 2, "share_in_plane"
+    )
+    total, peak, mass = exchange(total, peak, mass, column, False, 5, "share_in_column")
+    attended = (total / mass[:, None]).astype(jnp.bfloat16)
+    attended = attended.reshape(high_count, own_kv, seq_slots, GROUPS, new_count, HD)
     attended = jnp.transpose(attended, (0, 2, 4, 1, 3, 5)).reshape(-1, query_cols)
     shares = jnp.dot(attended, w_out, preferred_element_type=jnp.float32).astype(jnp.bfloat16)
-    shares = shares.reshape(req_count, local_reqs * new_count, model_width)
-    shares = lax.all_to_all(shares, "req", split_axis=0, concat_axis=0, tiled=True)
-    summed = jnp.sum(shares.astype(jnp.float32), axis=0)
+    shares = shares.reshape(req_count, 1, -1, model_width)
+    shares = jnp.broadcast_to(shares, (req_count, low_count) + shares.shape[2:])
+    shares = shares.reshape((req_count * low_count,) + shares.shape[2:])
+    shares = push([shares], plane, True, 4, "share_outputs")[0]
+    shares = shares.reshape(
+        req_count, low_count, high_count // req_count, seq_slots * new_count, model_width
+    )
+    summed = jnp.swapaxes(jnp.sum(shares.astype(jnp.float32), axis=0), 0, 1)
     out_hidden = (tokens_wide + summed.reshape(tokens_wide.shape)).astype(jnp.bfloat16)
 
     starts = my_lengths - seq_index * positions

time: 326 us -> 242 us (0.74)
  waiting for transfers between devices: 183 us -> 0.01 us
  Pallas kernels: 77.4 us -> 189 us
  blocking collectives: 12.3 us -> 0 us
  other arithmetic: 17.8 us -> 14.2 us
  starting transfers between devices: 4.21 us -> 7.61 us
    all_to_all x1, waiting for transfers between devices: 183 us -> 0.01 us  [shards(): lax.all_to_all(outgoing, ('req', 'seq'), split_axis=0, concat_axis=0, til...]
    pallas_call x5, Pallas kernels: 48 us -> 160 us  [push(): pl.pallas_call(functools.partial(push_kernel, tuple(digits), spread, len(...]
    all_to_all x1 -> x0, blocking collectives: 12.3 us -> none  [shards(): lax.all_to_all(shares, 'req', split_axis=0, concat_axis=0, tiled=True)]
    all_to_all x1, starting transfers between devices: 4.21 us -> 7.61 us  [shards(): lax.all_to_all(outgoing, ('req', 'seq'), split_axis=0, concat_axis=0, til...]
  transfers between devices with their start and end apart: 1 -> 1, of which waited for: 1 -> 0; matrix products, arithmetic and copies ran while one was open for 1% -> 11% of each run, Pallas kernels for 0% -> 72%
where the time goes in v5:
time: 242 us; the launch traced here: 239 us
  Pallas kernels  189 us (78%)
  local copies, waits for them, and re-layouts  21.9 us (9%)
  other arithmetic  14.2 us (6%)
  starting transfers between devices  7.61 us (3%)
  matrix products  5.15 us (2%)
    pallas_call x5, Pallas kernels, push(): pl.pallas_call(functools.partial(push_kernel, tuple(digits), spread, len(...  160 us
    pallas_call x1, Pallas kernels, attend(): pl.pallas_call(functools.partial(attend_kernel, new_count), grid=(KVH,),...  13.1 us
    pallas_call x1, Pallas kernels, collect(): pl.pallas_call(collect_kernel, in_specs=[pl.BlockSpec(memory_space=pltpu....  8.45 us
    pallas_call x1, Pallas kernels, place(): pl.pallas_call(place_kernel, in_specs=[smem, smem, vmem, vmem, whole], ou...  7.73 us
    all_to_all x1, starting transfers between devices, shards(): lax.all_to_all(outgoing, ('req', 'seq'), split_axis=0, concat_axis=0, til...  7.61 us
    dot_general x3, local copies, waits for them, and re-layouts, shards(): heads = lambda w: jnp.dot(flat_rows, w, preferred_element_type=jnp.float32)  6.38 us
    unnamed x20, local copies, waits for them, and re-layouts  5.13 us
  transfers between devices with their start and end apart: 1, of which 0 were waited for; matrix products, arithmetic and copies ran while one was open for 11% of the time, Pallas kernels for 72%

profile of v5, /device:TPU:0, one launch (start us, length us, event | category | flops | bytes accessed | tf_op | source)
XLA Modules:
  0.0 239.3 jit_solution(8793053036349823763)
XLA Ops:
  0.7 0.9 constant_dynamic-slice_fusion
  1.7 0.7 fusion.20
  2.3 0.8 select_reduce_fusion.3
  3.3 0.2 select_reduce_fusion.1
  3.6 0.5 and_select_fusion
  4.1 1.1 fusion.4
  5.2 1.0 fusion.6
  6.4 3.3 %select_reduce_fusion = s32[128]{0:T(128)S(1)} fusion(s32[32,128]{1,0:T(8,128)S(1)} %add_add_fusion, s32[32,128]{1,0:T(8,128)} %param.21, s32[128]{0:T(128)S(1)} %iota_add_fusion), kind=kLoop, calls=%fused_computation.1 | loop fusion | flops 1572736 | bytes 33792 | tf_op jit(solution)/shard_map/reduce_sum | solution.py:339
  9.6 0.2 convert_reduce_fusion.2
  9.8 0.1 select_reduce_fusion.2.order
  9.9 2.2 copy-done.1
  12.1 8.5 %collect_pages.1 = bf16[32,2,4,16,1024]{4,3,2,1,0:T(8,128)(2,1)} custom-call(s32[128]{0:T(128)S(1)} %select_reduce_fusion.2.order, bf16[128,16,1024]{2,1,0:T(8,128)(2,1)S(1)} %copy-done.1, bf16[128,16,1024]{2,1,0:T(8,128)(2,1)} %values.1), custom_call_target="tpu_custom_call" | custom-call | bytes 16777216 | tf_op jit(solution)/shard_map/collect_pages/pallas_call | solution.py:131
  20.6 7.6 %all-to-all-start = ((bf16[32,2,4,16,1024]{4,3,2,1,0:T(8,128)(2,1)}), bf16[32,2,4,16,1024]{4,3,2,1,0:T(8,128)(2,1)}, u32[]{:S(2)}, u32[]{:S(2)}) async-start(bf16[32,2,4,16,1024]{4,3,2,1,0:T(8,128)(2,1)} %collect_pages.1), calls=%async_computation | async-start | bytes 16777216 | tf_op jit(solution)/shard_map/all_to_all | solution.py:364
  28.3 0.1 select_reduce_fusion.4
  28.4 0.1 fusion.8
  28.5 0.1 select_n.176.page_info
  28.6 0.1 select_n.179.own_info
  28.7 72.1 %gather_tokens.1 = bf16[4,32,2048]{2,1,0:T(8,128)(2,1)S(1)} custom-call(bf16[32,2048]{1,0:T(8,128)(2,1)S(1)} %reshape.562.refs_0_), custom_call_target="tpu_custom_call" | custom-call | tf_op jit(solution)/shard_map/gather_tokens/pallas_call | solution.py:282
  100.8 2.3 copy.80
  103.1 0.2 dot_general.22
  103.3 0.3 multiply_cosine_fusion
  103.6 1.8 fusion
  105.4 0.1 subtract_convert_fusion.1
  105.5 0.1 pad_maximum_fusion.4
  105.7 3.9 %copy.77 = bf16[512,2048]{1,0:T(8,128)(2,1)} copy(bf16[512,2048]{0,1:T(8,128)(2,1)} %bitcast.87) | data formatting | bytes 4194304 | tf_op jit(solution)/shard_map/dot_general | solution.py:369
  109.6 2.5 %fusion.2 = f32[32,4,4,128]{3,0,2,1:T(8,128)S(1)} fusion(bf16[4,128,2048,1]{2,1,0,3:T(8,128)(2,1)} %bitcast.88, bf16[32,4,2048,1]{2,1,0,3:T(4,128)(2,1)S(1)} %bitcast.90), kind=kOutput, calls=%fused_computation.8 | convolution fusion | flops 268435456 | bytes 2883584 | tf_op jit(solution)/shard_map/dot_general | solution.py:369
  112.2 0.2 subtract_convert_fusion
  112.3 0.1 pad_maximum_fusion.3
  112.5 0.3 convolution_convert_fusion.1
  112.9 22.7 %gather_heads.1 = bf16[4,128,1024]{2,1,0:T(8,128)(2,1)S(1)} custom-call(bf16[128,1024]{1,0:T(8,128)(2,1)S(1)} %pad_maximum_fusion.refs_0_), custom_call_target="tpu_custom_call" | custom-call | tf_op jit(solution)/shard_map/gather_heads/pallas_call | solution.py:282
  135.6 0.8 slice.53
  136.4 2.0 reshape.566
  138.4 1.3 copy.63
  139.7 0.1 fusion.24
  139.9 13.1 %attend_held_pages.1 = (f32[8,256,128]{2,1,0:T(8,128)S(1)}, f32[8,256,1]{2,1,0:T(8,128)S(1)}, f32[8,256,1]{2,1,0:T(8,128)S(1)}) custom-call(s32[1,2048]{1,0:T(1,128)S(1)} %select_n.176.page_info, s32[1,128]{1,0:T(1,128)S(1)} %select_n.179.own_info, bf16[8,256,128]{2,1,0:T(8,128)(2,1)S(1)} %bitcast.78, bf16[2048,1024]{1,0:T(8,128)(2,1)} %bitcast.76, ...), custom_call_target="tpu_custom_call" | custom-call | flops 2147483648 | bytes 8388608 | tf_op jit(solution)/shard_map/attend_held_pages/pallas_call | solution.py:76
  153.0 1.0 copy-done.4
  154.0 0.9 copy-done.3
  154.9 0.9 copy.64
  155.8 1.6 reduce.5
  157.3 0.1 reshape_squeeze.7
  157.5 0.1 stack_reshape.7
  157.6 1.6 reduce.4
  159.1 0.1 reshape_squeeze.6
  159.3 0.1 stack_reshape.6
  159.4 1.0 copy-done.2
  160.4 14.8 %share_in_plane.1 = (bf16[8,256,128]{2,1,0:T(8,128)(2,1)S(1)}, f32[8,8,256]{2,1,0:T(8,128)S(1)}) custom-call(bf16[8,256,128]{2,1,0:T(8,128)(2,1)S(1)} %bitcast.79, f32[8,8,256]{2,1,0:T(8,128)S(1)} %select_maximum_fusion.refs_1_), custom_call_target="tpu_custom_call" | custom-call | tf_op jit(solution)/shard_map/share_in_plane/pallas_call | solution.py:282
  175.3 0.3 multiply_reduce_fusion.refs_0_
  175.7 41.2 %share_in_column.1 = (bf16[4,256,128]{2,1,0:T(8,128)(2,1)S(1)}, f32[4,8,256]{2,1,0:T(8,128)S(1)}) custom-call(bf16[256,128]{1,0:T(8,128)(2,1)S(1)} %multiply_reduce_fusion.refs_0_, f32[8,256]{1,0:T(8,128)S(1)} %select_maximum_fusion.1.refs_1_), custom_call_target="tpu_custom_call" | custom-call | tf_op jit(solution)/shard_map/share_in_column/pallas_call | solution.py:282
  217.0 0.1 div.94
  217.1 0.2 multiply_reduce_fusion.1
  217.3 0.1 fusion.10
  217.6 0.5 convolution_convert_fusion
  218.1 9.0 %share_outputs.1 = bf16[8,16,2048]{2,1,0:T(8,128)(2,1)S(1)} custom-call(bf16[8,16,2048]{2,1,0:T(8,128)(2,1)S(1)} %bitcast.80), custom_call_target="tpu_custom_call" | custom-call | tf_op jit(solution)/shard_map/share_outputs/pallas_call | solution.py:282
  227.1 0.1 convert_reduce_fusion
  227.2 0.8 reshape_transpose.3
  228.0 0.7 fusion.23
  228.7 0.2 copy.81
  229.0 0.1 reshape.581.fresh_keys
  229.1 1.2 copy.82
  230.2 0.1 reshape.582.fresh_values
  230.3 0.1 dynamic-slice_subtract_fusion.starts
  230.4 0.2 convert_reduce_fusion.1
  230.7 0.7 fusion.7
  231.4 7.7 %place_pages.1 = (bf16[128,16,1024]{2,1,0:T(8,128)(2,1)}, bf16[128,16,1024]{2,1,0:T(8,128)(2,1)}) custom-call(s32[256]{0:T(256)S(1)} %pad_add_fusion.placement, s32[8]{0:T(128)S(1)} %dynamic-slice_subtract_fusion.starts, f32[8,4,1024]{2,1,0:T(4,128)S(1)} %reshape.581.fresh_keys, f32[8,4,1024]{2,1,0:T(4,128)S(1)} %reshape.582.fresh_values, ...), custom_call_target="tpu_custom_call" | custom-call | bytes 16777216 | tf_op jit(solution)/shard_map/place_pages/pallas_call | solution.py:201
  (56 shorter events, 1.2 us)
Async XLA Ops:
  0.6 216.9 %copy-start = (bf16[512,2048]{1,0:T(8,128)(2,1)S(1)}, bf16[512,2048]{1,0:T(8,128)(2,1)}, u32[]{:S(2)}) copy-start(bf16[512,2048]{1,0:T(8,128)(2,1)} %param.16) | copy-start | bytes 6291460
  9.9 2.2 copy-start.1
  20.6 210.8 %all-to-all-start = ((bf16[32,2,4,16,1024]{4,3,2,1,0:T(8,128)(2,1)}), bf16[32,2,4,16,1024]{4,3,2,1,0:T(8,128)(2,1)}, u32[]{:S(2)}, u32[]{:S(2)}) async-start(bf16[32,2,4,16,1024]{4,3,2,1,0:T(8,128)(2,1)} %collect_pages.1), calls=%async_computation | async-start | bytes 16777216 | tf_op jit(solution)/shard_map/all_to_all | solution.py:364
  109.6 2.9 %copy-start.6 = (bf16[2048,256]{1,0:T(8,128)(2,1)S(1)}, bf16[2048,256]{1,0:T(8,128)(2,1)}, u32[]{:S(2)}) copy-start(bf16[2048,256]{1,0:T(8,128)(2,1)} %param.15) | copy-start | bytes 3145732
  153.0 1.0 copy-start.4
  153.9 1.0 copy-start.3
  159.4 1.0 copy-start.2
  227.1 3.3 %copy-start.8 = (s32[128]{0:T(128)S(1)}, s32[128]{0:T(128)}, u32[]{:S(2)}) copy-start(s32[128]{0:T(128)} %get-tuple-element.49) | copy-start | bytes 1540
  227.1 3.5 %copy-start.5 = (bf16[8,4,2048]{2,1,0:T(4,128)(2,1)S(1)}, bf16[8,4,2048]{2,1,0:T(4,128)(2,1)}, u32[]{:S(2)}) copy-start(bf16[8,4,2048]{2,1,0:T(4,128)(2,1)} %param.11) | copy-start | bytes 393220
  228.0 2.7 %copy-start.7 = (f32[8,4,2048]{2,1,0:T(4,128)S(1)}, f32[8,4,2048]{2,1,0:T(4,128)}, u32[]{:S(2)}) copy-start(f32[8,4,2048]{2,1,0:T(4,128)} %reshape_transpose.3) | copy-start | bytes 786436

commit v6 on v5

--- a/solution.py
+++ b/solution.py
@@ -435,6 +435,8 @@
 
     plane = [("req", 1, req_count), ("seq", 1, low_count)]
     column = [("seq", low_count, high_count)]
+    placing = (placement, my_lengths - seq_index * positions, of_mine(new_keys), of_mine(new_values))
+    total, placing = lax.optimization_barrier((total, placing))
     total, peak, mass = exchange(
         by_plane(total), by_plane(peak), by_plane(mass), plane, True, 2, "share_in_plane"
     )
@@ -453,11 +455,8 @@
     summed = jnp.swapaxes(jnp.sum(shares.astype(jnp.float32), axis=0), 0, 1)
     out_hidden = (tokens_wide + summed.reshape(tokens_wide.shape)).astype(jnp.bfloat16)
 
-    starts = my_lengths - seq_index * positions
     out_shape = (local_reqs, positions, kv_width)
-    keys_out, values_out = place(
-        placement, starts, of_mine(new_keys), of_mine(new_values), incoming
-    )
+    keys_out, values_out = place(*placing, incoming)
     return (out_hidden, keys_out.reshape(out_shape), values_out.reshape(out_shape))
 
 

time: 242 us -> 238 us (0.983)
  Pallas kernels: 189 us -> 184 us
    pallas_call x5, Pallas kernels: 160 us -> 155 us  [push(): pl.pallas_call(functools.partial(push_kernel, tuple(digits), spread, len(...]
    unnamed x20 -> x22, local copies, waits for them, and re-layouts: 5.13 us -> 5.42 us
  transfers between devices with their start and end apart: 1 -> 1, of which waited for: 0 -> 0; matrix products, arithmetic and copies ran while one was open for 11% -> 12% of each run, Pallas kernels for 72% -> 71%
where the time goes in v6:
time: 238 us; the launch traced here: 235 us
  Pallas kernels  184 us (77%)
  local copies, waits for them, and re-layouts  22.4 us (9%)
  other arithmetic  14.4 us (6%)
  starting transfers between devices  7.61 us (3%)
  matrix products  5.23 us (2%)
    pallas_call x5, Pallas kernels, push(): pl.pallas_call(functools.partial(push_kernel, tuple(digits), spread, len(...  155 us
    pallas_call x1, Pallas kernels, attend(): pl.pallas_call(functools.partial(attend_kernel, new_count), grid=(KVH,),...  13.1 us
    pallas_call x1, Pallas kernels, collect(): pl.pallas_call(collect_kernel, in_specs=[pl.BlockSpec(memory_space=pltpu....  8.45 us
    pallas_call x1, Pallas kernels, place(): pl.pallas_call(place_kernel, in_specs=[smem, smem, vmem, vmem, whole], ou...  7.67 us
    all_to_all x1, starting transfers between devices, shards(): lax.all_to_all(outgoing, ('req', 'seq'), split_axis=0, concat_axis=0, til...  7.61 us
    dot_general x3, local copies, waits for them, and re-layouts, shards(): heads = lambda w: jnp.dot(flat_rows, w, preferred_element_type=jnp.float32)  6.37 us
    unnamed x22, local copies, waits for them, and re-layouts  5.42 us
  transfers between devices with their start and end apart: 1, of which 0 were waited for; matrix products, arithmetic and copies ran while one was open for 12% of the time, Pallas kernels for 71%

profile of v6, /device:TPU:0, one launch (start us, length us, event | category | flops | bytes accessed | tf_op | source)
XLA Modules:
  0.0 235.3 jit_solution(9097995326709603761)
XLA Ops:
  0.7 0.9 constant_dynamic-slice_fusion
  1.7 0.7 fusion.20
  2.3 0.8 select_reduce_fusion.3
  3.3 0.2 select_reduce_fusion.1
  3.6 1.1 fusion.4
  4.7 1.0 fusion.6
  5.8 3.3 %select_reduce_fusion = s32[128]{0:T(128)S(1)} fusion(s32[32,128]{1,0:T(8,128)S(1)} %add_add_fusion, s32[32,128]{1,0:T(8,128)} %param.21, s32[128]{0:T(128)S(1)} %iota_add_fusion), kind=kLoop, calls=%fused_computation.1 | loop fusion | flops 1572736 | bytes 33792 | tf_op jit(solution)/shard_map/reduce_sum | solution.py:339
  9.1 0.2 convert_reduce_fusion.2
  9.3 0.1 select_reduce_fusion.2.order
  9.4 2.2 copy-done.1
  11.6 8.5 %collect_pages.1 = bf16[32,2,4,16,1024]{4,3,2,1,0:T(8,128)(2,1)} custom-call(s32[128]{0:T(128)S(1)} %select_reduce_fusion.2.order, bf16[128,16,1024]{2,1,0:T(8,128)(2,1)S(1)} %copy-done.1, bf16[128,16,1024]{2,1,0:T(8,128)(2,1)} %values.1), custom_call_target="tpu_custom_call" | custom-call | bytes 16777216 | tf_op jit(solution)/shard_map/collect_pages/pallas_call | solution.py:131
  20.1 7.6 %all-to-all-start = ((bf16[32,2,4,16,1024]{4,3,2,1,0:T(8,128)(2,1)}), bf16[32,2,4,16,1024]{4,3,2,1,0:T(8,128)(2,1)}, u32[]{:S(2)}, u32[]{:S(2)}) async-start(bf16[32,2,4,16,1024]{4,3,2,1,0:T(8,128)(2,1)} %collect_pages.1), calls=%async_computation | async-start | bytes 16777216 | tf_op jit(solution)/shard_map/all_to_all | solution.py:364
  27.8 0.1 select_reduce_fusion.4
  27.9 0.1 fusion.8
  28.0 0.1 select_n.176.page_info
  28.1 0.1 select_n.179.own_info
  28.2 72.1 %gather_tokens.1 = bf16[4,32,2048]{2,1,0:T(8,128)(2,1)S(1)} custom-call(bf16[32,2048]{1,0:T(8,128)(2,1)S(1)} %reshape.562.refs_0_), custom_call_target="tpu_custom_call" | custom-call | tf_op jit(solution)/shard_map/gather_tokens/pallas_call | solution.py:282
  100.3 2.3 copy.80
  102.6 0.2 dot_general.22
  102.8 0.3 multiply_cosine_fusion
  103.1 1.9 fusion
  105.0 0.1 subtract_convert_fusion.1
  105.1 0.1 pad_maximum_fusion.4
  105.3 0.6 copy.96
  105.9 3.9 %copy.77 = bf16[512,2048]{1,0:T(8,128)(2,1)} copy(bf16[512,2048]{0,1:T(8,128)(2,1)} %bitcast.87) | data formatting | bytes 4194304 | tf_op jit(solution)/shard_map/dot_general | solution.py:369
  109.8 2.5 %fusion.2 = f32[32,4,4,128]{3,0,2,1:T(8,128)S(1)} fusion(bf16[4,128,2048,1]{2,1,0,3:T(8,128)(2,1)} %bitcast.88, bf16[32,4,2048,1]{2,1,0,3:T(4,128)(2,1)S(1)} %bitcast.90), kind=kOutput, calls=%fused_computation.8 | convolution fusion | flops 268435456 | bytes 2883584 | tf_op jit(solution)/shard_map/dot_general | solution.py:369
  112.4 0.1 subtract_convert_fusion
  112.6 0.1 pad_maximum_fusion.3
  112.8 0.3 convolution_convert_fusion.1
  113.1 0.1 copy-done.9
  113.3 22.9 %gather_heads.1 = bf16[4,128,1024]{2,1,0:T(8,128)(2,1)S(1)} custom-call(bf16[128,1024]{1,0:T(8,128)(2,1)S(1)} %pad_maximum_fusion.refs_0_), custom_call_target="tpu_custom_call" | custom-call | tf_op jit(solution)/shard_map/gather_heads/pallas_call | solution.py:282
  136.2 0.8 slice.53
  137.0 2.0 reshape.566
  139.0 2.1 copy.63
  141.1 0.7 fusion.23
  141.8 0.2 copy.81
  142.1 0.1 reshape.580.fresh_keys
  142.2 1.2 copy.82
  143.3 0.7 convert_bitcast_fusion
  144.0 1.0 reshape.581.fresh_values
  145.0 0.1 dynamic-slice_subtract_fusion.starts
  145.1 0.2 convert_reduce_fusion.1
  145.3 0.1 fusion.24
  145.5 0.6 copy-done.2
  146.1 13.1 %attend_held_pages.1 = (f32[8,256,128]{2,1,0:T(8,128)S(1)}, f32[8,256,1]{2,1,0:T(8,128)S(1)}, f32[8,256,1]{2,1,0:T(8,128)S(1)}) custom-call(s32[1,2048]{1,0:T(1,128)S(1)} %select_n.176.page_info, s32[1,128]{1,0:T(1,128)S(1)} %select_n.179.own_info, bf16[8,256,128]{2,1,0:T(8,128)(2,1)S(1)} %bitcast.78, bf16[2048,1024]{1,0:T(8,128)(2,1)} %bitcast.76, ...), custom_call_target="tpu_custom_call" | custom-call | flops 2147483648 | bytes 8388608 | tf_op jit(solution)/shard_map/attend_held_pages/pallas_call | solution.py:76
  159.2 1.0 copy-done.4
  160.2 0.9 copy-done.3
  161.2 1.6 reduce.5
  162.8 0.1 reshape_squeeze.7
  162.9 0.1 stack_reshape.7
  163.0 1.6 reduce.4
  164.5 0.1 reshape_squeeze.6
  164.7 0.1 stack_reshape.6
  164.8 13.7 %share_in_plane.1 = (bf16[8,256,128]{2,1,0:T(8,128)(2,1)S(1)}, f32[8,8,256]{2,1,0:T(8,128)S(1)}) custom-call(bf16[8,256,128]{2,1,0:T(8,128)(2,1)S(1)} %bitcast.79, f32[8,8,256]{2,1,0:T(8,128)S(1)} %select_maximum_fusion.refs_1_), custom_call_target="tpu_custom_call" | custom-call | tf_op jit(solution)/shard_map/share_in_plane/pallas_call | solution.py:282
  178.6 0.3 multiply_reduce_fusion.refs_0_
  178.9 37.4 %share_in_column.1 = (bf16[4,256,128]{2,1,0:T(8,128)(2,1)S(1)}, f32[4,8,256]{2,1,0:T(8,128)S(1)}) custom-call(bf16[256,128]{1,0:T(8,128)(2,1)S(1)} %multiply_reduce_fusion.refs_0_, f32[8,256]{1,0:T(8,128)S(1)} %select_maximum_fusion.1.refs_1_), custom_call_target="tpu_custom_call" | custom-call | tf_op jit(solution)/shard_map/share_in_column/pallas_call | solution.py:282
  216.4 0.1 div.97
  216.6 0.2 multiply_reduce_fusion.1
  216.8 0.1 fusion.10
  217.0 0.5 convolution_convert_fusion
  217.6 9.0 %share_outputs.1 = bf16[8,16,2048]{2,1,0:T(8,128)(2,1)S(1)} custom-call(bf16[8,16,2048]{2,1,0:T(8,128)(2,1)S(1)} %bitcast.80), custom_call_target="tpu_custom_call" | custom-call | tf_op jit(solution)/shard_map/share_outputs/pallas_call | solution.py:282
  226.6 0.1 convert_reduce_fusion
  226.8 0.7 fusion.7
  227.5 7.7 %place_pages.1 = (bf16[128,16,1024]{2,1,0:T(8,128)(2,1)}, bf16[128,16,1024]{2,1,0:T(8,128)(2,1)}) custom-call(s32[256]{0:T(256)S(1)} %pad_add_fusion.placement, s32[8]{0:T(128)S(1)} %dynamic-slice_subtract_fusion.starts, f32[8,4,1024]{2,1,0:T(4,128)S(1)} %reshape.580.fresh_keys, f32[8,4,1024]{2,1,0:T(4,128)S(1)} %reshape.581.fresh_values, ...), custom_call_target="tpu_custom_call" | custom-call | bytes 16777216 | tf_op jit(solution)/shard_map/place_pages/pallas_call | solution.py:201
  (58 shorter events, 1.3 us)
Async XLA Ops:
  0.6 216.4 %copy-start = (bf16[512,2048]{1,0:T(8,128)(2,1)S(1)}, bf16[512,2048]{1,0:T(8,128)(2,1)}, u32[]{:S(2)}) copy-start(bf16[512,2048]{1,0:T(8,128)(2,1)} %param.16) | copy-start | bytes 6291460
  9.4 2.2 copy-start.1
  20.1 207.4 %all-to-all-start = ((bf16[32,2,4,16,1024]{4,3,2,1,0:T(8,128)(2,1)}), bf16[32,2,4,16,1024]{4,3,2,1,0:T(8,128)(2,1)}, u32[]{:S(2)}, u32[]{:S(2)}) async-start(bf16[32,2,4,16,1024]{4,3,2,1,0:T(8,128)(2,1)} %collect_pages.1), calls=%async_computation | async-start | bytes 16777216 | tf_op jit(solution)/shard_map/all_to_all | solution.py:364
  103.1 6.7 %copy-start.7 = (f32[32,4,64]{2,0,1:T(8,128)}, f32[32,4,64]{2,0,1:T(8,128)S(1)}, u32[]{:S(2)}) copy-start(f32[32,4,64]{2,0,1:T(8,128)S(1)} %get-tuple-element.56) | copy-start | bytes 98308
  109.8 2.6 %copy-start.8 = (f32[32,4,64]{2,0,1:T(8,128)S(1)}, f32[32,4,64]{2,0,1:T(8,128)}, u32[]{:S(2)}) copy-start(f32[32,4,64]{2,0,1:T(8,128)} %copy-done.7) | copy-start | bytes 98308
  109.8 3.0 %copy-start.6 = (bf16[2048,256]{1,0:T(8,128)(2,1)S(1)}, bf16[2048,256]{1,0:T(8,128)(2,1)}, u32[]{:S(2)}) copy-start(bf16[2048,256]{1,0:T(8,128)(2,1)} %param.15) | copy-start | bytes 3145732
  112.4 0.8 copy-start.9
  145.0 1.0 copy-start.2
  159.2 1.0 copy-start.4
  160.1 1.0 copy-start.3
  217.5 9.2 %copy-start.5 = (bf16[8,4,2048]{2,1,0:T(4,128)(2,1)S(1)}, bf16[8,4,2048]{2,1,0:T(4,128)(2,1)}, u32[]{:S(2)}) copy-start(bf16[8,4,2048]{2,1,0:T(4,128)(2,1)} %param.11) | copy-start | bytes 393220
